TPU v7x, 32 devices: a whole 2x2x4 slice. The times are simulated.
32 devices in a mesh: section: 2 (over x), dp: 4 (over y, core), tensor: 4 (over z).
Axes of the slice: x: 2, y: 2, z: 4, core: 2. Of those that a mesh axis runs over, the one named last changes fastest.
Arguments:
- ends_in: bfloat16 [2, 4, 2048, 768], P('section', None, ('dp', 'tensor')), may hold values from -6 to 6
- segments: int32 [4, 4, 512], P(None, 'dp'), may hold values from 0 to 3, as said below
- qkv_weight: bfloat16 [2, 2304, 768], P('section', ('tensor', 'dp')), may hold values from -0.21875 to 0.21875
- qkv_bias: bfloat16 [2, 2, 768], P('section', None, ('tensor', 'dp')), may hold values from -1.5 to 1.5
- output_weight: bfloat16 [2, 768, 768], P('section', ('tensor', 'dp')), may hold values from -0.875 to 0.875
- expand_weight: bfloat16 [2, 3072, 768], P('section', ('tensor', 'dp')), may hold values from -0.21875 to 0.21875
- expand_bias: bfloat16 [2, 3072], P('section', ('tensor', 'dp')), may hold values from -1.5 to 1.5
- contract_weight: bfloat16 [2, 3072, 768], P('section', ('tensor', 'dp')), may hold values from -0.109375 to 0.109375
- norm_gains: bfloat16 [2, 2, 768], P('section', None, 'dp'), may hold values from 0.5 to 1.5
- row_biases: bfloat16 [2, 4, 768], P('section', None, 'dp'), may hold values from -1.5 to 1.5
Outputs:
- ends_out: float32 [2, 4, 2048, 768], P('section', None, ('dp', 'tensor'))
- qkv_weight_grad: float32 [2, 2304, 768], P('section', ('tensor', 'dp'))
- qkv_bias_grad: float32 [2, 2, 768], P('section', None, ('tensor', 'dp'))
- output_weight_grad: float32 [2, 768, 768], P('section', ('tensor', 'dp'))
- expand_weight_grad: float32 [2, 3072, 768], P('section', ('tensor', 'dp'))
- expand_bias_grad: float32 [2, 3072], P('section', ('tensor', 'dp'))
- contract_weight_grad: float32 [2, 3072, 768], P('section', ('tensor', 'dp'))
- norm_gains_grad: float32 [2, 2, 768], P('section', None, 'dp')
- row_biases_grad: float32 [2, 4, 768], P('section', None, 'dp')
Inputs may be any that keep to these rules, and one draw needn't show every extreme that they name: `segments`: the sequences are consecutive cuts of one stream of documents in order (micro-batch, sequence); segment numbers count the documents met within a sequence from 0 and never fall along it.
All inputs are finite; a program needn't handle non-finite values.
Results may differ from a plain program's by a relative error of at most 0.03.
Values may be sent and summed in bfloat16 or wider, within the bound.
A program may use at most 128 MiB of HBM per device.

v0:
```python
from functools import partial

import jax
import jax.numpy as jnp
from jax import lax
from jax.sharding import PartitionSpec as P

HD = 64


EPS = 1e-05
MASKED = -1e30


def passed_along(x, axis, by):
    devices = lax.axis_size(axis)
    pairs = [(i, i + by) for i in range(devices) if 0 <= i + by < devices]
    return lax.ppermute(x, axis, pairs)


def norm_forward(hidden, gain_row, shift_row):
    average = jnp.mean(hidden, axis=-1, keepdims=True)
    centred = hidden - average
    variance = jnp.mean(centred * centred, axis=-1, keepdims=True)
    inverse = lax.rsqrt(variance + EPS)
    normed = centred * inverse
    return (normed * gain_row + shift_row, normed, inverse)


def norm_backward(grad_out, normed, inverse, gain_row):
    grad_normed = grad_out * gain_row
    inner_sum = jnp.mean(grad_normed, axis=-1, keepdims=True)
    along_norm = jnp.mean(grad_normed * normed, axis=-1, keepdims=True)
    grad_in = inverse * (grad_normed - inner_sum - normed * along_norm)
    return (grad_in, jnp.sum(grad_out * normed, axis=0), jnp.sum(grad_out, axis=0))


def gather_rows(row_block):
    return lax.all_gather(row_block, "tensor", axis=0, tiled=True)


def unit_sums(left_side, right_side):
    return lax.psum_scatter(
        jnp.dot(left_side, right_side, preferred_element_type=jnp.float32).astype(jnp.bfloat16),
        "tensor",
        scatter_dimension=0,
        tiled=True,
    ).astype(jnp.float32)


def split_heads(joined, segment_ids):
    seq_count, length = segment_ids.shape
    head_parts = joined.reshape(seq_count, length, -1, 3, HD)
    return (head_parts[:, :, :, 0], head_parts[:, :, :, 1], head_parts[:, :, :, 2])


def masked_scores(query_parts, key_parts, segment_ids):
    scores = jnp.einsum(
        "sqhe,skhe->shqk", query_parts, key_parts, preferred_element_type=jnp.float32
    ) * HD ** (-0.5)
    same_segment = (segment_ids[:, :, None] == segment_ids[:, None, :])[:, None]
    return (jnp.where(same_segment, scores, MASKED), same_segment)


def attend(joined, segment_ids):
    query_parts, key_parts, value_parts = split_heads(joined, segment_ids)
    scores, same_segment = masked_scores(query_parts, key_parts, segment_ids)
    row_peak = jnp.max(scores, axis=-1, keepdims=True)
    exp_scores = jnp.where(same_segment, jnp.exp(scores - row_peak), 0.0)
    row_total = jnp.sum(exp_scores, axis=-1, keepdims=True)
    soft_weights = (exp_scores / row_total).astype(jnp.bfloat16)
    context = jnp.einsum(
        "shqk,skhe->sqhe", soft_weights, value_parts, preferred_element_type=jnp.float32
    )
    logsum = row_peak + jnp.log(row_total)
    return (context.reshape(joined.shape[0], -1).astype(jnp.bfloat16), logsum)


def attend_back(joined, segment_ids, logsum, grad_context):
    query_parts, key_parts, value_parts = split_heads(joined, segment_ids)
    scores, same_segment = masked_scores(query_parts, key_parts, segment_ids)
    soft_float = jnp.where(same_segment, jnp.exp(scores - logsum), 0.0)
    soft_weights = soft_float.astype(jnp.bfloat16)
    grad_heads = grad_context.reshape(value_parts.shape)
    grad_values = jnp.einsum(
        "shqk,sqhe->skhe", soft_weights, grad_heads, preferred_element_type=jnp.float32
    )
    grad_soft = jnp.einsum(
        "sqhe,skhe->shqk", grad_heads, value_parts, preferred_element_type=jnp.float32
    )
    inner_sum = jnp.sum(grad_soft * soft_float, axis=-1, keepdims=True)
    grad_scores = (soft_float * (grad_soft - inner_sum)).astype(jnp.bfloat16)
    scale_factor = HD ** (-0.5)
    grad_query = (
        jnp.einsum("shqk,skhe->sqhe", grad_scores, key_parts, preferred_element_type=jnp.float32)
        * scale_factor
    )
    grad_keys = (
        jnp.einsum("shqk,sqhe->skhe", grad_scores, query_parts, preferred_element_type=jnp.float32)
        * scale_factor
    )
    stacked = jnp.stack([grad_query, grad_keys, grad_values], axis=3)
    return stacked.reshape(joined.shape).astype(jnp.bfloat16)


def layer_forward(inputs, segment_ids, weights):
    (
        qkv_weight,
        qkv_bias,
        output_weight,
        expand_weight,
        expand_bias,
        contract_weight,
        norm_gains,
        row_biases,
    ) = weights
    gains_float = norm_gains.astype(jnp.float32)
    biases_float = row_biases.astype(jnp.float32)
    rows_all = gather_rows(inputs)
    head_count = qkv_weight.shape[0] // (3 * HD)
    bias_float = qkv_bias.astype(jnp.float32)
    bias_parts = jnp.stack(
        [
            bias_float[0].reshape(head_count, HD),
            jnp.zeros((head_count, HD), jnp.float32),
            bias_float[1].reshape(head_count, HD),
        ],
        axis=1,
    ).reshape(-1)
    joined = (
        jnp.einsum("nd,md->nm", rows_all, qkv_weight, preferred_element_type=jnp.float32)
        + bias_parts
    ).astype(jnp.bfloat16)
    context, logsum = attend(joined, segment_ids)
    attended = unit_sums(context, output_weight)
    hidden_one = inputs.astype(jnp.float32) + attended + biases_float[0]
    first_out, normed_one, inverse_one = norm_forward(hidden_one, gains_float[0], biases_float[1])
    mid_rows = gather_rows(first_out.astype(jnp.bfloat16))
    pre_act = jnp.einsum(
        "nd,fd->nf", mid_rows, expand_weight, preferred_element_type=jnp.float32
    ) + expand_bias.astype(jnp.float32)
    activated = jax.nn.gelu(pre_act, approximate=False).astype(jnp.bfloat16)
    returned = unit_sums(activated, contract_weight)
    hidden_two = first_out + returned + biases_float[2]
    result, normed_two, inverse_two = norm_forward(hidden_two, gains_float[1], biases_float[3])
    saved_items = (
        rows_all,
        joined,
        logsum,
        context,
        normed_one,
        inverse_one,
        mid_rows,
        pre_act,
        activated,
        normed_two,
        inverse_two,
    )
    return (result, saved_items)


def layer_backward(grad_result, segment_ids, weights, saved_items):
    (
        qkv_weight,
        qkv_bias,
        output_weight,
        expand_weight,
        expand_bias,
        contract_weight,
        norm_gains,
        row_biases,
    ) = weights
    (
        rows_all,
        joined,
        logsum,
        context,
        normed_one,
        inverse_one,
        mid_rows,
        pre_act,
        activated,
        normed_two,
        inverse_two,
    ) = saved_items
    gains_float = norm_gains.astype(jnp.float32)
    grad_two, gain_two, shift_two = norm_backward(
        grad_result, normed_two, inverse_two, gains_float[1]
    )
    grad_rows_two = gather_rows(grad_two.astype(jnp.bfloat16))
    grad_activated = jnp.einsum(
        "nd,fd->nf", grad_rows_two, contract_weight, preferred_element_type=jnp.float32
    )
    gelu_pull = jax.vjp(partial(jax.nn.gelu, approximate=False), pre_act)[1]
    grad_pre = gelu_pull(grad_activated)[0].astype(jnp.bfloat16)
    contract_grad = jnp.einsum(
        "nf,nd->fd", activated, grad_rows_two, preferred_element_type=jnp.float32
    )
    expand_grad = jnp.einsum("nf,nd->fd", grad_pre, mid_rows, preferred_element_type=jnp.float32)
    expand_bias_grad = jnp.sum(grad_pre.astype(jnp.float32), axis=0)
    grad_first = grad_two + unit_sums(grad_pre, expand_weight)
    grad_one, gain_one, shift_one = norm_backward(
        grad_first, normed_one, inverse_one, gains_float[0]
    )
    grad_rows_one = gather_rows(grad_one.astype(jnp.bfloat16))
    grad_context = jnp.einsum(
        "nd,md->nm", grad_rows_one, output_weight, preferred_element_type=jnp.float32
    ).astype(jnp.bfloat16)
    output_grad = jnp.einsum(
        "nm,nd->md", context, grad_rows_one, preferred_element_type=jnp.float32
    )
    grad_joined = attend_back(joined, segment_ids, logsum, grad_context)
    qkv_grad = jnp.einsum("nm,nd->md", grad_joined, rows_all, preferred_element_type=jnp.float32)
    joined_sums = jnp.sum(grad_joined.astype(jnp.float32), axis=0).reshape(-1, 3, HD)
    qkv_bias_grad = jnp.stack([joined_sums[:, 0].reshape(-1), joined_sums[:, 2].reshape(-1)])
    grad_inputs = grad_one + unit_sums(grad_joined, qkv_weight)
    gain_grad = jnp.stack([gain_one, gain_two])
    bias_grad = jnp.stack(
        [jnp.sum(grad_one, axis=0), shift_one, jnp.sum(grad_two, axis=0), shift_two]
    )
    return (
        grad_inputs,
        (
            qkv_grad,
            qkv_bias_grad,
            output_grad,
            expand_grad,
            expand_bias_grad,
            contract_grad,
            gain_grad,
            bias_grad,
        ),
    )


def fetch_each(
    qkv_weight,
    qkv_bias,
    output_weight,
    expand_weight,
    expand_bias,
    contract_weight,
    norm_gains,
    row_biases,
):
    return (
        lax.all_gather(qkv_weight[0], "dp", axis=0, tiled=True),
        lax.all_gather(qkv_bias[0], "dp", axis=1, tiled=True),
        lax.all_gather(output_weight[0], "dp", axis=0, tiled=True),
        lax.all_gather(expand_weight[0], "dp", axis=0, tiled=True),
        lax.all_gather(expand_bias[0], "dp", axis=0, tiled=True),
        lax.all_gather(contract_weight[0], "dp", axis=0, tiled=True),
        lax.all_gather(norm_gains[0], "dp", axis=1, tiled=True),
        lax.all_gather(row_biases[0], "dp", axis=1, tiled=True),
    )


def reduce_each(grads):
    return (
        lax.psum_scatter(
            grads[0].astype(jnp.bfloat16), "dp", scatter_dimension=0, tiled=True
        ).astype(jnp.float32),
        lax.psum_scatter(
            grads[1].astype(jnp.bfloat16), "dp", scatter_dimension=1, tiled=True
        ).astype(jnp.float32),
        lax.psum_scatter(
            grads[2].astype(jnp.bfloat16), "dp", scatter_dimension=0, tiled=True
        ).astype(jnp.float32),
        lax.psum_scatter(
            grads[3].astype(jnp.bfloat16), "dp", scatter_dimension=0, tiled=True
        ).astype(jnp.float32),
        lax.psum_scatter(
            grads[4].astype(jnp.bfloat16), "dp", scatter_dimension=0, tiled=True
        ).astype(jnp.float32),
        lax.psum_scatter(
            grads[5].astype(jnp.bfloat16), "dp", scatter_dimension=0, tiled=True
        ).astype(jnp.float32),
        lax.psum_scatter(
            grads[6].astype(jnp.bfloat16), "dp", scatter_dimension=1, tiled=True
        ).astype(jnp.float32),
        lax.psum_scatter(
            grads[7].astype(jnp.bfloat16), "dp", scatter_dimension=1, tiled=True
        ).astype(jnp.float32),
    )


def shards(
    ends_in,
    segments,
    qkv_weight,
    qkv_bias,
    output_weight,
    expand_weight,
    expand_bias,
    contract_weight,
    norm_gains,
    row_biases,
):
    section_index = lax.axis_index("section")
    micro_count = ends_in.shape[1]
    tick_count = micro_count + 1
    own_rows = ends_in[0]
    arriving = jnp.zeros(own_rows.shape[1:], jnp.bfloat16)
    results = []
    saved_list = []
    for tick_index in range(tick_count):
        batch_index = jnp.clip(tick_index - section_index, 0, micro_count - 1)
        inputs = jnp.where(section_index == 0, own_rows[min(tick_index, micro_count - 1)], arriving)
        segment_ids = lax.dynamic_index_in_dim(segments, batch_index, 0, keepdims=False)
        weights = fetch_each(
            qkv_weight,
            qkv_bias,
            output_weight,
            expand_weight,
            expand_bias,
            contract_weight,
            norm_gains,
            row_biases,
        )
        result, saved_items = layer_forward(inputs, segment_ids, weights)
        results.append(result)
        saved_list.append(saved_items)
        if tick_index + 1 < tick_count:
            arriving = passed_along(result.astype(jnp.bfloat16), "section", 1)
    totals = None
    arriving_grad = jnp.zeros(own_rows.shape[1:], jnp.bfloat16)
    input_grads = []
    for tick_index in range(tick_count):
        position = tick_index - 1 + section_index
        is_valid = (position >= 0) & (position < micro_count)
        batch_index = jnp.clip(position, 0, micro_count - 1)
        incoming = jnp.where(
            section_index == 1, own_rows[min(tick_index, micro_count - 1)], arriving_grad
        )
        incoming = jnp.where(is_valid, incoming.astype(jnp.float32), 0.0)
        segment_ids = lax.dynamic_index_in_dim(segments, batch_index, 0, keepdims=False)
        early_items = saved_list[max(tick_index - 1, 0)]
        later_items = saved_list[min(tick_index + 1, tick_count - 1)]
        saved_items = tuple(
            (
                jnp.where(section_index == 0, early_item, later_item)
                for early_item, later_item in zip(early_items, later_items)
            )
        )
        weights = fetch_each(
            qkv_weight,
            qkv_bias,
            output_weight,
            expand_weight,
            expand_bias,
            contract_weight,
            norm_gains,
            row_biases,
        )
        grad_inputs, grads = layer_backward(incoming, segment_ids, weights, saved_items)
        input_grads.append(grad_inputs)
        if tick_index + 1 < tick_count:
            arriving_grad = passed_along(grad_inputs.astype(jnp.bfloat16), "section", -1)
        step_grads = reduce_each(grads)
        if totals is None:
            totals = step_grads
        else:
            totals = tuple(
                (left_item + right_item for left_item, right_item in zip(totals, step_grads))
            )
    gain_total, bias_total = lax.psum((totals[6], totals[7]), "tensor")
    input_part = jnp.stack(input_grads[1:])
    output_part = jnp.stack(
        [
            lax.optimization_barrier(item.astype(jnp.bfloat16)).astype(jnp.float32)
            for item in results[1:]
        ]
    )
    ends_out = jnp.where(section_index == 0, input_part, output_part)[None]
    return (
        ends_out,
        totals[0][None],
        totals[1][None],
        totals[2][None],
        totals[3][None],
        totals[4][None],
        totals[5][None],
        gain_total[None],
        bias_total[None],
    )


def solution(mesh):
    in_specs = (
        P("section", None, ("dp", "tensor"), None),
        P(None, "dp", None),
        P("section", ("tensor", "dp"), None),
        P("section", None, ("tensor", "dp")),
        P("section", ("tensor", "dp"), None),
        P("section", ("tensor", "dp"), None),
        P("section", ("tensor", "dp")),
        P("section", ("tensor", "dp"), None),
        P("section", None, "dp"),
        P("section", None, "dp"),
    )
    out_specs = (
        P("section", None, ("dp", "tensor"), None),
        P("section", ("tensor", "dp"), None),
        P("section", None, ("tensor", "dp")),
        P("section", ("tensor", "dp"), None),
        P("section", ("tensor", "dp"), None),
        P("section", ("tensor", "dp")),
        P("section", ("tensor", "dp"), None),
        P("section", None, "dp"),
        P("section", None, "dp"),
    )
    return jax.shard_map(shards, mesh=mesh, in_specs=in_specs, out_specs=out_specs, check_vma=False)
```

profile of v0, /device:TPU:0, one launch (start us, length us, event | category | flops | bytes accessed | tf_op | source)
XLA Modules:
  0.0 1945.6 jit_solution(7294598739318922123)
XLA Ops:
  185.9 23.7 %reduce-scatter.90.cloned.1.call-done = bf16[128,768]{1,0:T(8,128)(2,1)} async-done(((bf16[512,768]{1,0:T(8,128)(2,1)}), bf16[128,768]{1,0:T(8,128)(2,1)}) %reduce-scatter.90.cloned.1.call-update) | async-done | bytes 196624 | tf_op jit(solution)/shard_map/reduce_scatter | solution.py:43
  296.3 23.6 %reduce-scatter.94.cloned.1.call-done = bf16[128,768]{1,0:T(8,128)(2,1)} async-done(((bf16[512,768]{1,0:T(8,128)(2,1)}), bf16[128,768]{1,0:T(8,128)(2,1)}) %reduce-scatter.94.cloned.1.call-update) | async-done | bytes 196624 | tf_op jit(solution)/shard_map/reduce_scatter | solution.py:43
  444.7 22.7 %reduce-scatter.98.cloned.1.call-done = bf16[128,768]{1,0:T(8,128)(2,1)} async-done(((bf16[512,768]{1,0:T(8,128)(2,1)}), bf16[128,768]{1,0:T(8,128)(2,1)}) %reduce-scatter.98.cloned.1.call-update) | async-done | bytes 196624 | tf_op jit(solution)/shard_map/reduce_scatter | solution.py:43
  607.2 27.5 %all_gather.72 = bf16[512,768]{1,0:T(8,128)(2,1)S(1)} all-gather(bf16[128,768]{1,0:T(8,128)(2,1)S(1)} %get-tuple-element.104), channel_id=1, replica_groups=mesh['section'=2,'dp'=4,'tensor'=4] {'tensor'}, dimensions={0}, use_global_device_ids=true | all-gather | bytes 983040 | tf_op jit(solution)/shard_map/all_gather | solution.py:39
  693.8 22.7 %reduce-scatter.104.cloned.1.call-done = bf16[128,768]{1,0:T(8,128)(2,1)} async-done(((bf16[512,768]{1,0:T(8,128)(2,1)}), bf16[128,768]{1,0:T(8,128)(2,1)}) %reduce-scatter.104.cloned.1.call-update) | async-done | bytes 196624 | tf_op jit(solution)/shard_map/reduce_scatter | solution.py:43
  1426.5 22.8 %reduce-scatter.140.cloned.1.call-done = bf16[48,768]{1,0:T(8,128)(2,1)} async-done(((bf16[192,768]{1,0:T(8,128)(2,1)}), bf16[48,768]{1,0:T(8,128)(2,1)}) %reduce-scatter.140.cloned.1.call-update) | async-done | bytes 73744 | tf_op jit(solution)/shard_map/reduce_scatter | solution.py:266
  1449.2 22.8 %reduce-scatter.142.cloned.1.call-done = bf16[48,768]{1,0:T(8,128)(2,1)} async-done(((bf16[192,768]{1,0:T(8,128)(2,1)}), bf16[48,768]{1,0:T(8,128)(2,1)}) %reduce-scatter.142.cloned.1.call-update) | async-done | bytes 73744 | tf_op jit(solution)/shard_map/reduce_scatter | solution.py:266
  1472.0 22.8 %reduce-scatter.144.cloned.1.call-done = bf16[48,768]{1,0:T(8,128)(2,1)} async-done(((bf16[192,768]{1,0:T(8,128)(2,1)}), bf16[48,768]{1,0:T(8,128)(2,1)}) %reduce-scatter.144.cloned.1.call-update) | async-done | bytes 73744 | tf_op jit(solution)/shard_map/reduce_scatter | solution.py:266
  1496.5 26.6 %reduce-scatter.156.cloned.1.call-done = bf16[192,768]{1,0:T(8,128)(2,1)} async-done(((bf16[768,768]{1,0:T(8,128)(2,1)}), bf16[192,768]{1,0:T(8,128)(2,1)}) %reduce-scatter.156.cloned.1.call-update) | async-done | bytes 294928 | tf_op jit(solution)/shard_map/reduce_scatter | solution.py:275
  1523.1 28.5 %reduce-scatter.158.cloned.1.call-done = bf16[192,768]{1,0:T(8,128)(2,1)} async-done(((bf16[768,768]{1,0:T(8,128)(2,1)}), bf16[192,768]{1,0:T(8,128)(2,1)}) %reduce-scatter.158.cloned.1.call-update) | async-done | bytes 294928 | tf_op jit(solution)/shard_map/reduce_scatter | solution.py:275
  1551.6 28.3 %reduce-scatter.160.cloned.1.call-done = bf16[192,768]{1,0:T(8,128)(2,1)} async-done(((bf16[768,768]{1,0:T(8,128)(2,1)}), bf16[192,768]{1,0:T(8,128)(2,1)}) %reduce-scatter.160.cloned.1.call-update) | async-done | bytes 294928 | tf_op jit(solution)/shard_map/reduce_scatter | solution.py:275
  1579.9 28.3 %reduce-scatter.162.cloned.1.call-done = bf16[192,768]{1,0:T(8,128)(2,1)} async-done(((bf16[768,768]{1,0:T(8,128)(2,1)}), bf16[192,768]{1,0:T(8,128)(2,1)}) %reduce-scatter.162.cloned.1.call-update) | async-done | bytes 294928 | tf_op jit(solution)/shard_map/reduce_scatter | solution.py:275
  1608.2 28.3 %reduce-scatter.164.cloned.1.call-done = bf16[192,768]{1,0:T(8,128)(2,1)} async-done(((bf16[768,768]{1,0:T(8,128)(2,1)}), bf16[192,768]{1,0:T(8,128)(2,1)}) %reduce-scatter.164.cloned.1.call-update) | async-done | bytes 294928 | tf_op jit(solution)/shard_map/reduce_scatter | solution.py:275
  1638.8 26.0 %reduce-scatter.146.cloned.1.call-done = bf16[192,768]{1,0:T(8,128)(2,1)} async-done(((bf16[768,768]{1,0:T(8,128)(2,1)}), bf16[192,768]{1,0:T(8,128)(2,1)}) %reduce-scatter.146.cloned.1.call-update) | async-done | bytes 294928 | tf_op jit(solution)/shard_map/reduce_scatter | solution.py:269
  1664.8 28.1 %reduce-scatter.148.cloned.1.call-done = bf16[192,768]{1,0:T(8,128)(2,1)} async-done(((bf16[768,768]{1,0:T(8,128)(2,1)}), bf16[192,768]{1,0:T(8,128)(2,1)}) %reduce-scatter.148.cloned.1.call-update) | async-done | bytes 294928 | tf_op jit(solution)/shard_map/reduce_scatter | solution.py:269
  1692.9 28.3 %reduce-scatter.150.cloned.1.call-done = bf16[192,768]{1,0:T(8,128)(2,1)} async-done(((bf16[768,768]{1,0:T(8,128)(2,1)}), bf16[192,768]{1,0:T(8,128)(2,1)}) %reduce-scatter.150.cloned.1.call-update) | async-done | bytes 294928 | tf_op jit(solution)/shard_map/reduce_scatter | solution.py:269
  1721.3 28.1 %reduce-scatter.152.cloned.1.call-done = bf16[192,768]{1,0:T(8,128)(2,1)} async-done(((bf16[768,768]{1,0:T(8,128)(2,1)}), bf16[192,768]{1,0:T(8,128)(2,1)}) %reduce-scatter.152.cloned.1.call-update) | async-done | bytes 294928 | tf_op jit(solution)/shard_map/reduce_scatter | solution.py:269
  1749.4 28.9 %reduce-scatter.154.cloned.1.call-done = bf16[192,768]{1,0:T(8,128)(2,1)} async-done(((bf16[768,768]{1,0:T(8,128)(2,1)}), bf16[192,768]{1,0:T(8,128)(2,1)}) %reduce-scatter.154.cloned.1.call-update) | async-done | bytes 294928 | tf_op jit(solution)/shard_map/reduce_scatter | solution.py:269
  1780.6 23.3 %reduce-scatter.124.cloned.1.call-done = bf16[128,768]{1,0:T(8,128)(2,1)} async-done(((bf16[512,768]{1,0:T(8,128)(2,1)}), bf16[128,768]{1,0:T(8,128)(2,1)}) %reduce-scatter.124.cloned.1.call-update) | async-done | bytes 196624 | tf_op jit(solution)/shard_map/reduce_scatter | solution.py:43
  1806.3 23.2 %reduce-scatter.126.cloned.1.call-done = bf16[144,768]{1,0:T(8,128)(2,1)} async-done(((bf16[576,768]{1,0:T(8,128)(2,1)}), bf16[144,768]{1,0:T(8,128)(2,1)}) %reduce-scatter.126.cloned.1.call-update) | async-done | bytes 221200 | tf_op jit(solution)/shard_map/reduce_scatter | solution.py:260
  1829.5 26.6 %reduce-scatter.128.cloned.1.call-done = bf16[144,768]{1,0:T(8,128)(2,1)} async-done(((bf16[576,768]{1,0:T(8,128)(2,1)}), bf16[144,768]{1,0:T(8,128)(2,1)}) %reduce-scatter.128.cloned.1.call-update) | async-done | bytes 221200 | tf_op jit(solution)/shard_map/reduce_scatter | solution.py:260
  1856.1 26.3 %reduce-scatter.130.cloned.1.call-done = bf16[144,768]{1,0:T(8,128)(2,1)} async-done(((bf16[576,768]{1,0:T(8,128)(2,1)}), bf16[144,768]{1,0:T(8,128)(2,1)}) %reduce-scatter.130.cloned.1.call-update) | async-done | bytes 221200 | tf_op jit(solution)/shard_map/reduce_scatter | solution.py:260
  1882.4 26.6 %reduce-scatter.132.cloned.1.call-done = bf16[144,768]{1,0:T(8,128)(2,1)} async-done(((bf16[576,768]{1,0:T(8,128)(2,1)}), bf16[144,768]{1,0:T(8,128)(2,1)}) %reduce-scatter.132.cloned.1.call-update) | async-done | bytes 221200 | tf_op jit(solution)/shard_map/reduce_scatter | solution.py:260
  1909.0 26.5 %reduce-scatter.134.cloned.1.call-done = bf16[144,768]{1,0:T(8,128)(2,1)} async-done(((bf16[576,768]{1,0:T(8,128)(2,1)}), bf16[144,768]{1,0:T(8,128)(2,1)}) %reduce-scatter.134.cloned.1.call-update) | async-done | bytes 221200 | tf_op jit(solution)/shard_map/reduce_scatter | solution.py:260
  (1024 shorter events, 1303.8 us)
Async XLA Ops:
  1045.5 290.8 %reduce-scatter.174.cloned.1.call-start = ((), (), s32[]{:S(2)}) async-start(), calls=%async_computation.101 | async-start | bytes 61440
  1077.7 280.8 %reduce-scatter.184.cloned.1.call-start = ((), (), s32[]{:S(2)}) async-start(), calls=%async_computation.106 | async-start | bytes 245760
  1079.3 301.5 %reduce-scatter.194.cloned.1.call-start = ((), (), s32[]{:S(2)}) async-start(), calls=%async_computation.111 | async-start | bytes 245760
  1080.3 323.5 %reduce-scatter.136.cloned.1.call-start = ((), (), s32[]{:S(2)}) async-start(), calls=%async_computation.80 | async-start | bytes 368640 | tf_op jit(solution)/shard_map/reduce_scatter | solution.py:266
  1081.4 345.0 %reduce-scatter.138.cloned.1.call-start = ((), (), s32[]{:S(2)}) async-start(), calls=%async_computation.81 | async-start | bytes 368640 | tf_op jit(solution)/shard_map/reduce_scatter | solution.py:266
  1082.6 366.6 %reduce-scatter.140.cloned.1.call-start = ((), (), s32[]{:S(2)}) async-start(), calls=%async_computation.82 | async-start | bytes 368640 | tf_op jit(solution)/shard_map/reduce_scatter | solution.py:266
  1083.8 388.2 %reduce-scatter.142.cloned.1.call-start = ((), (), s32[]{:S(2)}) async-start(), calls=%async_computation.83 | async-start | bytes 368640 | tf_op jit(solution)/shard_map/reduce_scatter | solution.py:266
  1085.0 409.8 %reduce-scatter.144.cloned.1.call-start = ((), (), s32[]{:S(2)}) async-start(), calls=%async_computation.84 | async-start | bytes 368640 | tf_op jit(solution)/shard_map/reduce_scatter | solution.py:266
  1086.2 437.0 %reduce-scatter.156.cloned.1.call-start = ((), (), s32[]{:S(2)}) async-start(), calls=%async_computation.90 | async-start | bytes 1474560 | tf_op jit(solution)/shard_map/reduce_scatter | solution.py:275
  1089.3 462.3 %reduce-scatter.158.cloned.1.call-start = ((), (), s32[]{:S(2)}) async-start(), calls=%async_computation.91 | async-start | bytes 1474560 | tf_op jit(solution)/shard_map/reduce_scatter | solution.py:275
  1092.5 487.4 %reduce-scatter.160.cloned.1.call-start = ((), (), s32[]{:S(2)}) async-start(), calls=%async_computation.92 | async-start | bytes 1474560 | tf_op jit(solution)/shard_map/reduce_scatter | solution.py:275
  1094.5 513.7 %reduce-scatter.162.cloned.1.call-start = ((), (), s32[]{:S(2)}) async-start(), calls=%async_computation.93 | async-start | bytes 1474560 | tf_op jit(solution)/shard_map/reduce_scatter | solution.py:275
  1097.6 538.8 %reduce-scatter.164.cloned.1.call-start = ((), (), s32[]{:S(2)}) async-start(), calls=%async_computation.94 | async-start | bytes 1474560 | tf_op jit(solution)/shard_map/reduce_scatter | solution.py:275
  1100.8 564.0 %reduce-scatter.146.cloned.1.call-start = ((), (), s32[]{:S(2)}) async-start(), calls=%async_computation.85 | async-start | bytes 1474560 | tf_op jit(solution)/shard_map/reduce_scatter | solution.py:269
  1103.9 589.0 %reduce-scatter.148.cloned.1.call-start = ((), (), s32[]{:S(2)}) async-start(), calls=%async_computation.86 | async-start | bytes 1474560 | tf_op jit(solution)/shard_map/reduce_scatter | solution.py:269
  1107.0 614.3 %reduce-scatter.150.cloned.1.call-start = ((), (), s32[]{:S(2)}) async-start(), calls=%async_computation.87 | async-start | bytes 1474560 | tf_op jit(solution)/shard_map/reduce_scatter | solution.py:269
  1110.4 639.0 %reduce-scatter.152.cloned.1.call-start = ((), (), s32[]{:S(2)}) async-start(), calls=%async_computation.88 | async-start | bytes 1474560 | tf_op jit(solution)/shard_map/reduce_scatter | solution.py:269
  1113.6 664.8 %reduce-scatter.154.cloned.1.call-start = ((), (), s32[]{:S(2)}) async-start(), calls=%async_computation.89 | async-start | bytes 1474560 | tf_op jit(solution)/shard_map/reduce_scatter | solution.py:269
  1116.6 687.3 %reduce-scatter.124.cloned.1.call-start = ((), (), s32[]{:S(2)}) async-start(), calls=%async_computation.74 | async-start | bytes 983040 | tf_op jit(solution)/shard_map/reduce_scatter | solution.py:43
  1119.7 709.8 %reduce-scatter.126.cloned.1.call-start = ((), (), s32[]{:S(2)}) async-start(), calls=%async_computation.75 | async-start | bytes 1105920 | tf_op jit(solution)/shard_map/reduce_scatter | solution.py:260
  1121.4 734.7 %reduce-scatter.128.cloned.1.call-start = ((), (), s32[]{:S(2)}) async-start(), calls=%async_computation.76 | async-start | bytes 1105920 | tf_op jit(solution)/shard_map/reduce_scatter | solution.py:260
  1124.2 758.2 %reduce-scatter.130.cloned.1.call-start = ((), (), s32[]{:S(2)}) async-start(), calls=%async_computation.77 | async-start | bytes 1105920 | tf_op jit(solution)/shard_map/reduce_scatter | solution.py:260
  1127.1 782.0 %reduce-scatter.132.cloned.1.call-start = ((), (), s32[]{:S(2)}) async-start(), calls=%async_computation.78 | async-start | bytes 1105920 | tf_op jit(solution)/shard_map/reduce_scatter | solution.py:260
  1129.8 805.7 %reduce-scatter.134.cloned.1.call-start = ((), (), s32[]{:S(2)}) async-start(), calls=%async_computation.79 | async-start | bytes 1105920 | tf_op jit(solution)/shard_map/reduce_scatter | solution.py:260
  (286 other events, 10808.5 us)
Sparse Core Ops, SparseCore 0:
  186.0 23.5 reduce-scatter.89
  240.6 22.5 reduce-scatter.91
  296.4 23.5 reduce-scatter.93
  349.7 22.5 reduce-scatter.95
  600.6 33.6 reduce-scatter.113
  693.9 22.5 reduce-scatter.103
  805.5 22.5 reduce-scatter.115
  856.3 22.5 reduce-scatter.111
  1497.4 25.7 reduce-scatter.155
  1525.9 25.6 reduce-scatter.157
  1554.2 25.6 reduce-scatter.159
  1582.5 25.6 reduce-scatter.161
  1610.7 25.6 reduce-scatter.163
  1639.1 25.6 reduce-scatter.145
  1667.2 25.6 reduce-scatter.147
  1695.5 25.7 reduce-scatter.149
  1723.7 25.6 reduce-scatter.151
  1752.6 25.6 reduce-scatter.153
  1780.6 23.2 reduce-scatter.123
  1806.4 23.0 reduce-scatter.125
  1832.2 23.8 reduce-scatter.127
  1858.5 23.8 reduce-scatter.129
  1885.1 23.8 reduce-scatter.131
  1911.6 23.8 reduce-scatter.133
  (31 shorter events, 638.0 us)
Sparse Core Ops, SparseCore 1:
  63.1 15.7 all-gather.11
  80.3 17.3 all-gather.13
where the time goes:
time: 1950 us
  waiting for transfers between devices  1130 us (58%)
  blocking collectives  437 us (22%)
  matrix products  178 us (9%)
  other arithmetic  85.9 us (4%)
  local copies, waits for them, and re-layouts  72.3 us (4%)
  starting transfers between devices  22.4 us (1%)
  between operations  21.4 us (1%)
    all_gather x20, blocking collectives, gather_rows(): return lax.all_gather(row_block, 'tensor', axis=0, tiled=True)  373 us
    reduce_scatter x20, waiting for transfers between devices, unit_sums(): lax.psum_scatter(jnp.dot(left_side, right_side, preferred_element_type=jn...  364 us
    unnamed x72, waiting for transfers between devices  227 us
    reduce_scatter x5, waiting for transfers between devices, reduce_each(): lax.psum_scatter(grads[5].astype(jnp.bfloat16), 'dp', scatter_dimension=0...  140 us
    reduce_scatter x5, waiting for transfers between devices, reduce_each(): lax.psum_scatter(grads[3].astype(jnp.bfloat16), 'dp', scatter_dimension=0...  140 us
    reduce_scatter x5, waiting for transfers between devices, reduce_each(): lax.psum_scatter(grads[0].astype(jnp.bfloat16), 'dp', scatter_dimension=0...  129 us
    reduce_scatter x5, waiting for transfers between devices, reduce_each(): lax.psum_scatter(grads[2].astype(jnp.bfloat16), 'dp', scatter_dimension=0...  101 us
    unnamed x526, local copies, waits for them, and re-layouts  45.3 us
  transfers between devices with their start and end apart: 65, of which 56 were waited for; matrix products, arithmetic and copies ran while one was open for 8% of the time, Pallas kernels for 0%

commit v1 on v0

v1 whole, which is shorter than its diff:
```python
import jax
import jax.numpy as jnp
from jax import lax
from jax.sharding import PartitionSpec as P

HD = 64
EPS = 1e-05
MASKED = -1e30
F32 = jnp.float32
BF16 = jnp.bfloat16
SHARDS = ("tensor", "dp")


def rows_by_units(left_side, right_side):
    return lax.dot_general(
        left_side, right_side, (((1,), (1,)), ((), ())), preferred_element_type=F32
    )


def over_rows(left_side, right_side):
    return lax.dot_general(
        left_side, right_side, (((0,), (0,)), ((), ())), preferred_element_type=F32
    )


def plain(left_side, right_side):
    return jnp.dot(left_side, right_side, preferred_element_type=F32)


def norm_forward(hidden, gain_row, shift_row):
    average = jnp.mean(hidden, axis=-1, keepdims=True)
    centred = hidden - average
    variance = jnp.mean(centred * centred, axis=-1, keepdims=True)
    inverse = lax.rsqrt(variance + EPS)
    normed = centred * inverse
    return (normed * gain_row + shift_row, normed, inverse)


def norm_backward(grad_out, normed, inverse, gain_row):
    grad_normed = grad_out * gain_row
    inner_sum = jnp.mean(grad_normed, axis=-1, keepdims=True)
    along_norm = jnp.mean(grad_normed * normed, axis=-1, keepdims=True)
    return inverse * (grad_normed - inner_sum - normed * along_norm)


def attend(joined, segment_ids):
    parts = joined.reshape(joined.shape[0], -1, 3, HD)
    query, key, value = parts[:, :, 0], parts[:, :, 1], parts[:, :, 2]
    scores = jnp.einsum("qhe,khe->hqk", query, key, preferred_element_type=F32) * HD ** (-0.5)
    same = (segment_ids[:, None] == segment_ids[None, :])[None]
    scores = jnp.where(same, scores, MASKED)
    peak = jnp.max(scores, axis=-1, keepdims=True)
    powers = jnp.exp(scores - peak)
    total = jnp.sum(powers, axis=-1, keepdims=True)
    soft = (powers / total).astype(BF16)
    context = jnp.einsum("hqk,khe->qhe", soft, value, preferred_element_type=F32)
    return (context.reshape(joined.shape[0], -1).astype(BF16), soft)


def attend_back(joined, soft, grad_context):
    parts = joined.reshape(joined.shape[0], -1, 3, HD)
    query, key, value = parts[:, :, 0], parts[:, :, 1], parts[:, :, 2]
    grad_heads = grad_context.reshape(value.shape)
    grad_value = jnp.einsum("hqk,qhe->khe", soft, grad_heads, preferred_element_type=F32)
    grad_soft = jnp.einsum("qhe,khe->hqk", grad_heads, value, preferred_element_type=F32)
    soft_float = soft.astype(F32)
    inner_sum = jnp.sum(grad_soft * soft_float, axis=-1, keepdims=True)
    grad_scores = (soft_float * (grad_soft - inner_sum)).astype(BF16)
    grad_query = jnp.einsum("hqk,khe->qhe", grad_scores, key, preferred_element_type=F32)
    grad_key = jnp.einsum("hqk,qhe->khe", grad_scores, query, preferred_element_type=F32)
    scale = HD ** (-0.5)
    stacked = jnp.stack([grad_query * scale, grad_key * scale, grad_value], axis=2)
    return stacked.reshape(joined.shape).astype(BF16)


def gelu_pair(pre_act):
    cdf = 0.5 * (1.0 + lax.erf(pre_act * 0.5**0.5))
    density = jnp.exp(-0.5 * pre_act * pre_act) * 0.3989422804014327
    return (pre_act * cdf, cdf + pre_act * density)


def layer_forward(inputs, segment_ids, weights, smalls):
    qkv, output, expand, contract = weights
    qkv_bias, expand_bias, gains, biases = smalls
    joined = (rows_by_units(inputs, qkv) + qkv_bias).astype(BF16)
    context, soft = attend(joined, segment_ids)
    hidden_one = inputs.astype(F32) + plain(context, output) + biases[0]
    first, normed_one, inverse_one = norm_forward(hidden_one, gains[0], biases[1])
    mid_rows = first.astype(BF16)
    pre_act = rows_by_units(mid_rows, expand) + expand_bias
    activated, slope = gelu_pair(pre_act)
    activated = activated.astype(BF16)
    hidden_two = first + plain(activated, contract) + biases[2]
    result, normed_two, inverse_two = norm_forward(hidden_two, gains[1], biases[3])
    saved = (
        joined,
        soft,
        context,
        normed_one,
        inverse_one,
        mid_rows,
        activated,
        slope.astype(BF16),
        normed_two,
        inverse_two,
    )
    return (result.astype(BF16), saved)


def layer_backward(grad_result, weights, gains, saved):
    qkv, output, expand, contract = weights
    joined, soft, context, normed_one, inverse_one, mid_rows, activated, slope, normed_two, inverse_two = saved
    grad_result = grad_result.astype(F32)
    grad_two = norm_backward(grad_result, normed_two, inverse_two, gains[1])
    grad_returned = grad_two.astype(BF16)
    grad_pre = (rows_by_units(grad_returned, contract) * slope.astype(F32)).astype(BF16)
    grad_first = grad_two + plain(grad_pre, expand)
    grad_one = norm_backward(grad_first, normed_one, inverse_one, gains[0])
    grad_attended = grad_one.astype(BF16)
    grad_context = rows_by_units(grad_attended, output).astype(BF16)
    grad_joined = attend_back(joined, soft, grad_context)
    grad_inputs = grad_one + plain(grad_joined, qkv)
    return (
        grad_inputs.astype(BF16),
        (grad_result, grad_two, grad_returned, grad_pre, grad_first, grad_one, grad_attended, grad_joined),
    )


def weight_scatter(grad):
    return lax.psum_scatter(grad.astype(BF16), SHARDS, scatter_dimension=0, tiled=True).astype(F32)


def shards(
    ends_in,
    segments,
    qkv_weight,
    qkv_bias,
    output_weight,
    expand_weight,
    expand_bias,
    contract_weight,
    norm_gains,
    row_biases,
):
    section = lax.axis_index("section")
    along = lax.axis_index("tensor")
    dp_at = lax.axis_index("dp")
    dp_count = lax.axis_size("dp")
    tensor_count = lax.axis_size("tensor")
    flat_count = dp_count * tensor_count
    features = ends_in.shape[-1]
    heads = features // HD
    bias_part = qkv_bias.shape[-1]
    unit_part = expand_bias.shape[-1]
    norm_part = norm_gains.shape[-1]

    own = lax.all_to_all(ends_in[0], "tensor", 0, 1, tiled=True)[0]
    packed = jnp.concatenate(
        [qkv_bias[0].reshape(-1), expand_bias[0], norm_gains[0].reshape(-1), row_biases[0].reshape(-1)]
    )
    packed = lax.all_gather(packed, SHARDS, axis=0, tiled=False).astype(F32)
    weights = tuple(
        lax.all_gather(item[0], SHARDS, axis=0, tiled=True)
        for item in (qkv_weight, output_weight, expand_weight, contract_weight)
    )
    cut_one = 2 * bias_part
    cut_two = cut_one + unit_part
    cut_three = cut_two + 2 * norm_part
    biases_qv = packed[:, :cut_one].reshape(flat_count, 2, bias_part).transpose(1, 0, 2).reshape(2, heads, HD)
    qkv_bias_row = jnp.stack(
        [biases_qv[0], jnp.zeros((heads, HD), F32), biases_qv[1]], axis=1
    ).reshape(-1)
    expand_bias_row = packed[:, cut_one:cut_two].reshape(-1)
    gains = packed[:dp_count, cut_two:cut_three].reshape(dp_count, 2, norm_part).transpose(1, 0, 2).reshape(2, features)
    biases = packed[:dp_count, cut_three:].reshape(dp_count, 4, norm_part).transpose(1, 0, 2).reshape(4, features)
    smalls = (qkv_bias_row, expand_bias_row, gains, biases)
    segment_ids = lax.dynamic_index_in_dim(segments, along, 0, keepdims=False)[0]

    early_result, _ = layer_forward(own, segment_ids, weights, smalls)
    arriving = lax.ppermute(early_result, "section", [(0, 1)])
    inputs = jnp.where(section == 0, own, arriving)
    result, saved = layer_forward(inputs, segment_ids, weights, smalls)
    early_grad, _ = layer_backward(own, weights, gains, saved)
    arriving_grad = lax.ppermute(early_grad, "section", [(1, 0)])
    cotangent = jnp.where(section == 1, own, arriving_grad)
    grad_inputs, items = layer_backward(cotangent, weights, gains, saved)
    grad_result, grad_two, grad_returned, grad_pre, grad_first, grad_one, grad_attended, grad_joined = items
    joined, soft, context, normed_one, inverse_one, mid_rows, activated, slope, normed_two, inverse_two = saved

    contract_grad = weight_scatter(over_rows(activated, grad_returned))
    expand_grad = weight_scatter(over_rows(grad_pre, mid_rows))
    output_grad = weight_scatter(over_rows(context, grad_attended))
    qkv_grad = weight_scatter(over_rows(grad_joined, inputs))
    joined_sums = jnp.sum(grad_joined.astype(F32), axis=0).reshape(heads, 3, HD)
    small_grads = jnp.concatenate(
        [
            joined_sums[:, 0].reshape(-1),
            joined_sums[:, 2].reshape(-1),
            jnp.sum(grad_first * normed_one, axis=0),
            jnp.sum(grad_result * normed_two, axis=0),
            jnp.sum(grad_one, axis=0),
            jnp.sum(grad_first, axis=0),
            jnp.sum(grad_two, axis=0),
            jnp.sum(grad_result, axis=0),
            jnp.sum(grad_pre.astype(F32), axis=0),
        ]
    )
    small_sums = lax.psum(small_grads, SHARDS)
    flat_at = along * dp_count + dp_at
    table = small_sums[: 8 * features].reshape(8, features)
    qkv_bias_grad = lax.dynamic_slice_in_dim(table[:2], flat_at * bias_part, bias_part, 1)
    norm_grads = lax.dynamic_slice_in_dim(table[2:], dp_at * norm_part, norm_part, 1)
    expand_bias_grad = lax.dynamic_slice_in_dim(
        small_sums[8 * features :], flat_at * unit_part, unit_part, 0
    )
    ends = jnp.where(section == 0, grad_inputs, result).reshape(ends_in.shape[1:])
    ends_out = lax.all_to_all(ends, "tensor", 0, 0, tiled=True).astype(F32)
    return (
        ends_out[None],
        qkv_grad[None],
        qkv_bias_grad[None],
        output_grad[None],
        expand_grad[None],
        expand_bias_grad[None],
        contract_grad[None],
        norm_grads[:2][None],
        norm_grads[2:][None],
    )


def solution(mesh):
    rows = P("section", None, ("dp", "tensor"), None)
    units = P("section", SHARDS, None)
    biases = P("section", None, SHARDS)
    norms = P("section", None, "dp")
    vector = P("section", SHARDS)
    return jax.shard_map(
        shards,
        mesh=mesh,
        in_specs=(rows, P(None, "dp", None), units, biases, units, units, vector, units, norms, norms),
        out_specs=(rows, units, biases, units, units, vector, units, norms, norms),
        check_vma=False,
    )
```

time: 1950 us -> 662 us (0.34)
  waiting for transfers between devices: 1130 us -> 282 us
  blocking collectives: 437 us -> 142 us
  other arithmetic: 85.9 us -> 35 us
  matrix products: 178 us -> 132 us
  local copies, waits for them, and re-layouts: 72.3 us -> 29 us
    reduce_scatter x40 -> x4, waiting for transfers between devices: 873 us -> 152 us  [weight_scatter(): lax.psum_scatter(grad.astype(BF16), SHARDS, scatter_dimension=0, tiled=True)]
    all_gather x25 -> x0, blocking collectives: 408 us -> none  [the longest x20 373 us: gather_rows(): return lax.all_gather(row_block, 'tensor', axis=0, tiled=True)]
    unnamed x72 -> x8, waiting for transfers between devices: 227 us -> 2.65 us
    all_gather x2 -> x4, waiting for transfers between devices: 0.01 us -> 91.3 us  [shards(): lax.all_gather(item[0], SHARDS, axis=0, tiled=True)]
    dot_general x95 -> x30, matrix products: 178 us -> 117 us  [the longest x8 40.4 us: rows_by_units(): lax.dot_general(left_side, right_side, (((1,), (1,)), ((), ())), preferre...]
    unnamed x2 -> x1, blocking collectives: 16.2 us -> 73.6 us
    psum x1, blocking collectives: 12.5 us -> 68.2 us  [shards(): small_sums = lax.psum(small_grads, SHARDS)]
    reduce_sum x34 -> x6, other arithmetic: 39.7 us -> 4.81 us  [the longest x1 2.62 us: shards(): jnp.sum(grad_result * normed_two, axis=0)]
  transfers between devices with their start and end apart: 65 -> 12, of which waited for: 56 -> 6; matrix products, arithmetic and copies ran while one was open for 8% -> 14% of each run, Pallas kernels for 0% -> 0%
where the time goes in v1:
time: 662 us; the launch traced here: 652 us
  waiting for transfers between devices  282 us (43%)
  blocking collectives  142 us (21%)
  matrix products  132 us (20%)
  other arithmetic  35 us (5%)
  local copies, waits for them, and re-layouts  29 us (4%)
  between operations  16.2 us (2%)
  starting transfers between devices  15.5 us (2%)
    reduce_scatter x4, waiting for transfers between devices, weight_scatter(): lax.psum_scatter(grad.astype(BF16), SHARDS, scatter_dimension=0, tiled=True)  152 us
    all_gather x4, waiting for transfers between devices, shards(): lax.all_gather(item[0], SHARDS, axis=0, tiled=True)  91.3 us
    unnamed x1, blocking collectives  73.6 us
    psum x1, blocking collectives, shards(): small_sums = lax.psum(small_grads, SHARDS)  68.2 us
    dot_general x8, matrix products, rows_by_units(): lax.dot_general(left_side, right_side, (((1,), (1,)), ((), ())), preferre...  40.4 us
    dot_general x8, matrix products, plain(): return jnp.dot(left_side, right_side, preferred_element_type=F32)  27.5 us
    ppermute x1, waiting for transfers between devices, shards(): arriving_grad = lax.ppermute(early_grad, 'section', [(1, 0)])  19.9 us
    dot_general x4, matrix products, over_rows(): lax.dot_general(left_side, right_side, (((0,), (0,)), ((), ())), preferre...  19.2 us
  transfers between devices with their start and end apart: 12, of which 6 were waited for; matrix products, arithmetic and copies ran while one was open for 14% of the time, Pallas kernels for 0%

profile of v1, /device:TPU:0, one launch (start us, length us, event | category | flops | bytes accessed | tf_op | source)
XLA Modules:
  0.0 652.2 jit_solution(11802294874830134033)
XLA Ops:
  10.0 6.3 all-to-all-start
  18.3 73.6 %all-reduce = bf16[23040]{0:T(1024)(128)(2,1)S(1)} all-reduce(bf16[23040]{0:T(1024)(128)(2,1)S(1)} %dynamic-update-slice), channel_id=3, replica_groups=mesh['section'=2,'dp'=4,'tensor'=4] {'tensor','dp'}, use_global_device_ids=true, to_apply=%add | all-reduce | flops 23040 | bytes 92160
  93.9 5.7 fusion.36
  102.5 7.6 %fusion.118 = (f32[12,512]{1,0:T(8,128)S(1)}, f32[12,512,512]{1,2,0:T(8,128)}) fusion(pred[512,512]{0,1:T(8,128)(4,1)S(1)} %broadcast_compare_fusion, bf16[512,12,3,64]{0,3,2,1:T(8,128)(2,1)S(1)} %bitcast.268), kind=kOutput, calls=%fused_computation.209 | convolution fusion | flops 415236608 | bytes 14442496 | tf_op jit(solution)/shard_map/sub | solution.py:53
  110.1 6.7 %fusion.72 = bf16[12,64,512]{2,1,0:T(8,128)(2,1)} fusion(f32[12,512,512]{1,2,0:T(8,128)} %get-tuple-element.39, f32[12,512]{1,0:T(8,128)S(1)} %get-tuple-element.38, bf16[512,12,3,64]{0,3,2,1:T(8,128)(2,1)S(1)} %bitcast.269), kind=kOutput, calls=%fused_computation.118 | convolution fusion | flops 409337856 | bytes 14188544 | tf_op jit(solution)/shard_map/hqk,khe->qhe/dot_general | solution.py:56
  119.6 43.9 %all-gather.14.cloned.1.call-done = bf16[1,3072,768]{2,1,0:T(8,128)(2,1)} async-done(((bf16[1,192,768]{2,1,0:T(8,128)(2,1)}), bf16[1,3072,768]{2,1,0:T(8,128)(2,1)}) %all-gather.14.cloned.1.call-update) | async-done | bytes 4718608 | tf_op jit(solution)/shard_map/all_gather | solution.py:163
  163.5 6.7 %multiply_convert_fusion.1 = bf16[512,3072]{1,0:T(8,128)(2,1)} fusion(bf16[1,3072,768]{2,1,0:T(8,128)(2,1)} %all-gather.14.cloned.1.call-done, f32[3072]{0:T(1024)S(1)} %add.199, f32[512,768]{1,0:T(8,128)S(1)} %get-tuple-element.41, f32[768]{0:T(1024)S(1)} %add.196, f32[768]{0:T(1024)S(1)} %mul.279, f32[512]{0:T(512)S(1)} %add_rsqrt_fusion.3, ...), kind=kOutput, calls=%fused_computation.31 | convolution fusion | flops 2427322368 | bytes 9459712 | tf_op jit(solution)/shard_map/dot_general | solution.py:15
  170.2 47.4 %all-gather.16.cloned.1.call-done = bf16[1,3072,768]{2,1,0:T(8,128)(2,1)} async-done(((bf16[1,192,768]{2,1,0:T(8,128)(2,1)}), bf16[1,3072,768]{2,1,0:T(8,128)(2,1)}) %all-gather.16.cloned.1.call-update) | async-done | bytes 4718608 | tf_op jit(solution)/shard_map/all_gather | solution.py:163
  217.6 6.1 fusion.120
  228.2 16.7 %collective-permute-done = bf16[512,768]{1,0:T(8,128)(2,1)S(1)} collective-permute-done((bf16[512,768]{1,0:T(8,128)(2,1)S(1)}, bf16[512,768]{1,0:T(8,128)(2,1)S(1)}, u32[]{:S(2)}, u32[]{:S(2)}) %collective-permute-start) | collective-permute-done | bytes 786464 | tf_op jit(solution)/shard_map/ppermute | solution.py:180
  246.0 5.5 fusion.37
  254.3 7.6 %fusion.121 = (f32[12,512]{1,0:T(8,128)S(1)}, f32[12,512,512]{1,2,0:T(8,128)}) fusion(pred[512,512]{0,1:T(8,128)(4,1)S(1)} %broadcast_compare_fusion, bf16[512,12,3,64]{0,3,2,1:T(8,128)(2,1)S(1)} %bitcast.250), kind=kOutput, calls=%fused_computation.212 | convolution fusion | flops 415236608 | bytes 14442496 | tf_op jit(solution)/shard_map/sub | solution.py:53
  261.9 6.4 divide_convert_fusion
  273.5 7.4 %fusion.14 = (bf16[512,3072]{1,0:T(8,128)(2,1)S(1)}, bf16[512,3072]{1,0:T(8,128)(2,1)S(1)}) fusion(f32[3072]{0:T(1024)S(1)} %add.199, bf16[1,3072,768]{2,1,0:T(8,128)(2,1)} %all-gather.14.cloned.1.call-done, f32[768]{0:T(1024)S(1)} %add.196, f32[768]{0:T(1024)S(1)} %mul.279, f32[512]{0:T(512)S(1)} %add_rsqrt_fusion.1, ...), kind=kOutput, calls=%fused_computation.27 | convolution fusion | flops 2436759552 | bytes 12605440 | tf_op jit(solution)/shard_map/dot_general | solution.py:15
  303.3 6.3 fusion.3
  322.4 19.9 %collective-permute-done.1 = bf16[512,768]{1,0:T(8,128)(2,1)} collective-permute-done((bf16[512,768]{1,0:T(8,128)(2,1)}, bf16[512,768]{1,0:T(8,128)(2,1)}, u32[]{:S(2)}, u32[]{:S(2)}) %collective-permute-start.1) | collective-permute-done | bytes 786464 | tf_op jit(solution)/shard_map/ppermute | solution.py:184
  345.6 6.3 convert_reduce_fusion
  368.7 6.4 fusion.5
  387.5 6.7 %convolution_convert_fusion = bf16[3072,768]{1,0:T(8,128)(2,1)} fusion(bf16[512,3072]{1,0:T(8,128)(2,1)} %copy-done.36, f32[512,768]{1,0:T(8,128)S(1)} %copy-done.21), kind=kOutput, calls=%fused_computation.39 | convolution fusion | flops 2418671616 | bytes 9437184 | tf_op jit(solution)/shard_map/dot_general | solution.py:21
  395.7 6.9 %convolution_convert_fusion.1 = bf16[3072,768]{1,0:T(8,128)(2,1)} fusion(bf16[512,3072]{1,0:T(8,128)(2,1)} %copy-done.38, f32[768]{0:T(1024)S(1)} %add.196, f32[768]{0:T(1024)S(1)} %mul.279, f32[512,768]{1,0:T(8,128)S(1)} %copy-done.18, f32[512]{0:T(512)S(1)} %add_rsqrt_fusion.1, f32[512]{0:T(512)S(1)} %broadcast_multiply_fusion.8), kind=kOutput, calls=%fused_computation.40 | convolution fusion | flops 2420244480 | bytes 9447424 | tf_op jit(solution)/shard_map/dot_general | solution.py:21
  404.4 5.9 fusion.81
  414.0 68.2 %psum.7 = f32[9216]{0:T(1024)S(1)} all-reduce(f32[9216]{0:T(1024)S(1)} %constant_dynamic-update-slice_fusion), channel_id=1, replica_groups=mesh['section'=2,'dp'=4,'tensor'=4] {'tensor','dp'}, use_global_device_ids=true, to_apply=%region_31.32 | all-reduce | flops 9216 | bytes 73728 | tf_op jit(solution)/shard_map/psum | solution.py:208
  489.4 74.7 %reduce-scatter.11.cloned.1.call-done = bf16[192,768]{1,0:T(8,128)(2,1)} async-done(((bf16[3072,768]{1,0:T(8,128)(2,1)}), bf16[192,768]{1,0:T(8,128)(2,1)}) %reduce-scatter.11.cloned.1.call-update) | async-done | bytes 294928 | tf_op jit(solution)/shard_map/reduce_scatter | solution.py:130
  565.9 77.2 %reduce-scatter.9.cloned.1.call-done = bf16[192,768]{1,0:T(8,128)(2,1)} async-done(((bf16[3072,768]{1,0:T(8,128)(2,1)}), bf16[192,768]{1,0:T(8,128)(2,1)}) %reduce-scatter.9.cloned.1.call-update) | async-done | bytes 294928 | tf_op jit(solution)/shard_map/reduce_scatter | solution.py:130
  (244 shorter events, 109.8 us)
Async XLA Ops:
  7.2 86.4 %copy-start = (s32[4,1,512]{2,1,0:T(1,128)S(1)}, s32[4,1,512]{2,1,0:T(1,128)}, u32[]{:S(2)}) copy-start(s32[4,1,512]{2,1,0:T(1,128)} %param.11) | copy-start | bytes 24580
  7.2 10.6 %copy-start.29 = (bf16[1,192]{1,0:T(2,128)(2,1)S(1)}, bf16[1,192]{1,0:T(2,128)(2,1)}, u32[]{:S(2)}) copy-start(bf16[1,192]{1,0:T(2,128)(2,1)} %param.16) | copy-start | bytes 1156
  7.2 86.6 %all-gather.10.cloned.1.call-start = ((), (), s32[]{:S(2)}) async-start(), calls=%async_computation.10 | async-start | bytes 3760128 | tf_op jit(solution)/shard_map/all_gather | solution.py:163
  8.0 108.8 %all-gather.12.cloned.1.call-start = ((), (), s32[]{:S(2)}) async-start(), calls=%async_computation.11 | async-start | bytes 1253376 | tf_op jit(solution)/shard_map/all_gather | solution.py:163
  8.7 154.8 %all-gather.14.cloned.1.call-start = ((), (), s32[]{:S(2)}) async-start(), calls=%async_computation.12 | async-start | bytes 5013504 | tf_op jit(solution)/shard_map/all_gather | solution.py:163
  9.5 208.2 %all-gather.16.cloned.1.call-start = ((), (), s32[]{:S(2)}) async-start(), calls=%async_computation.13 | async-start | bytes 5013504 | tf_op jit(solution)/shard_map/all_gather | solution.py:163
  10.0 83.8 %all-to-all-start = ((bf16[4,128,768]{2,1,0:T(8,128)(2,1)}), bf16[4,128,768]{2,1,0:T(8,128)(2,1)S(1)}, u32[]{:S(2)}, u32[]{:S(2)}) async-start(bf16[4,128,768]{2,1,0:T(8,128)(2,1)} %bitcast.271), calls=%async_computation | async-start | bytes 1572864 | tf_op jit(solution)/shard_map/all_to_all | solution.py:157
  16.4 469.7 %reduce-scatter.7.cloned.1.call-start = ((), (), s32[]{:S(2)}) async-start(), calls=%async_computation.7 | async-start | bytes 1253376 | tf_op jit(solution)/shard_map/reduce_scatter | solution.py:130
  93.6 130.4 %copy-start.25 = (f32[768]{0:T(1024)}, f32[768]{0:T(1024)S(1)}, u32[]{:S(2)}) copy-start(f32[768]{0:T(1024)S(1)} %add.208) | copy-start | bytes 9220
  93.8 151.1 %copy-start.8 = (bf16[4,128,768]{2,1,0:T(8,128)(2,1)}, bf16[4,128,768]{2,1,0:T(8,128)(2,1)S(1)}, u32[]{:S(2)}) copy-start(bf16[4,128,768]{2,1,0:T(8,128)(2,1)S(1)} %all-to-all-done) | copy-start | bytes 2359300
  224.3 20.6 %collective-permute-start = (bf16[512,768]{1,0:T(8,128)(2,1)S(1)}, bf16[512,768]{1,0:T(8,128)(2,1)S(1)}, u32[]{:S(2)}, u32[]{:S(2)}) collective-permute-start(bf16[512,768]{1,0:T(8,128)(2,1)S(1)} %add_convert_fusion.3), channel_id=1, source_target_pairs={{0,16},{1,17},{2,18},{3,19},{4,20},{5,21},{6,22},{7,23},{8,24},{9,... | collective-permute-start | bytes 2359304 | tf_op jit(solution)/shard_map/ppermute | solution.py:180
  273.1 19.7 %copy-start.15 = (f32[512,768]{1,0:T(8,128)}, f32[512,768]{1,0:T(8,128)S(1)}, u32[]{:S(2)}) copy-start(f32[512,768]{1,0:T(8,128)S(1)} %get-tuple-element.47) | copy-start | bytes 4718596
  298.3 14.5 %slice-start = ((s8[6291456]{0:T(1024)(128)(4,1)}), s8[4194304]{0:T(1024)(128)(4,1)S(1)}, s32[]{:S(2)}) async-start(s8[6291456]{0:T(1024)(128)(4,1)} %bitcast.246), calls=%async_computation.14 | async-start | bytes 8388608
  303.3 9.5 %slice-start.1 = ((s8[6291456]{0:T(1024)(128)(4,1)}), s8[2097152]{0:T(1024)(128)(4,1)S(1)}, s32[]{:S(2)}) async-start(s8[6291456]{0:T(1024)(128)(4,1)} %bitcast.246), calls=%async_computation.15 | async-start | bytes 4194304
  321.1 21.2 %collective-permute-start.1 = (bf16[512,768]{1,0:T(8,128)(2,1)}, bf16[512,768]{1,0:T(8,128)(2,1)}, u32[]{:S(2)}, u32[]{:S(2)}) collective-permute-start(bf16[512,768]{1,0:T(8,128)(2,1)} %add_convert_fusion.2), channel_id=1, source_target_pairs={{16,0},{17,1},{18,2},{19,3},{20,4},{21,5},{22,6},{23,7},{24,8},{25... | collective-permute-start | bytes 2359304 | tf_op jit(solution)/shard_map/ppermute | solution.py:184
  322.4 22.6 %copy-start.6 = (f32[512,768]{1,0:T(8,128)S(1)}, f32[512,768]{1,0:T(8,128)}, u32[]{:S(2)}) copy-start(f32[512,768]{1,0:T(8,128)} %copy-done.5) | copy-start | bytes 4718596
  342.3 9.6 %slice-start.6 = ((s8[4718592]{0:T(1024)(128)(4,1)}), s8[4194304]{0:T(1024)(128)(4,1)S(1)}, s32[]{:S(2)}) async-start(s8[4718592]{0:T(1024)(128)(4,1)} %bitcast.280), calls=%async_computation.20 | async-start | bytes 8388608
  358.6 129.1 %reduce-scatter.5.cloned.1.call-start = ((), (), s32[]{:S(2)}) async-start(), calls=%async_computation.6 | async-start | bytes 3760128 | tf_op jit(solution)/shard_map/reduce_scatter | solution.py:130
  363.8 14.5 %slice-start.2 = ((s8[6291456]{0:T(1024)(128)(4,1)}), s8[4194304]{0:T(1024)(128)(4,1)S(1)}, s32[]{:S(2)}) async-start(s8[6291456]{0:T(1024)(128)(4,1)} %bitcast.248), calls=%async_computation.16 | async-start | bytes 8388608
  368.7 9.6 %slice-start.3 = ((s8[6291456]{0:T(1024)(128)(4,1)}), s8[2097152]{0:T(1024)(128)(4,1)S(1)}, s32[]{:S(2)}) async-start(s8[6291456]{0:T(1024)(128)(4,1)} %bitcast.248), calls=%async_computation.17 | async-start | bytes 4194304
  386.2 177.9 %reduce-scatter.11.cloned.1.call-start = ((), (), s32[]{:S(2)}) async-start(), calls=%async_computation.9 | async-start | bytes 5013504 | tf_op jit(solution)/shard_map/reduce_scatter | solution.py:130
  394.3 248.8 %reduce-scatter.9.cloned.1.call-start = ((), (), s32[]{:S(2)}) async-start(), calls=%async_computation.8 | async-start | bytes 5013504 | tf_op jit(solution)/shard_map/reduce_scatter | solution.py:130
  410.3 74.5 %all-to-all-start.1 = ((bf16[4,128,768]{2,1,0:T(8,128)(2,1)}), bf16[4,128,768]{2,1,0:T(8,128)(2,1)S(1)}, u32[]{:S(2)}, u32[]{:S(2)}) async-start(bf16[4,128,768]{2,1,0:T(8,128)(2,1)} %bitcast.272), calls=%async_computation.1 | async-start | bytes 1572864 | tf_op jit(solution)/shard_map/all_to_all | solution.py:217
  484.8 160.1 %copy-start.1 = (s32[4,1,512]{2,1,0:T(1,128)S(1)}, s32[4,1,512]{2,1,0:T(1,128)}, u32[]{:S(2)}) copy-start(s32[4,1,512]{2,1,0:T(1,128)} %param.11) | copy-start | bytes 24580
  (37 other events, 142.9 us)
Sparse Core Ops, SparseCore 0:
  10.4 59.2 all-gather.9
  71.9 36.8 all-gather.11
  111.1 52.3 all-gather.13
  165.6 51.9 all-gather.15
  358.7 55.7 reduce-scatter.6
  418.2 67.5 reduce-scatter.4
  489.7 74.3 reduce-scatter.10
  568.4 74.5 reduce-scatter.8

commit v2 on v1

v2 whole, which is shorter than its diff:
```python
from functools import partial

import jax
import jax.numpy as jnp
from jax import lax
from jax.experimental import pallas as pl
from jax.experimental.pallas import tpu as pltpu
from jax.sharding import PartitionSpec as P

HD = 64
EPS = 1e-05
MASKED = -1e30
F32 = jnp.float32
BF16 = jnp.bfloat16
SHARDS = ("tensor", "dp")


def rows_by_units(left_side, right_side):
    return lax.dot_general(
        left_side, right_side, (((1,), (1,)), ((), ())), preferred_element_type=F32
    )


def over_rows(left_side, right_side):
    return lax.dot_general(
        left_side, right_side, (((0,), (0,)), ((), ())), preferred_element_type=F32
    )


def plain(left_side, right_side):
    return jnp.dot(left_side, right_side, preferred_element_type=F32)


def norm_forward(hidden, gain_row, shift_row):
    average = jnp.mean(hidden, axis=-1, keepdims=True)
    centred = hidden - average
    variance = jnp.mean(centred * centred, axis=-1, keepdims=True)
    inverse = lax.rsqrt(variance + EPS)
    normed = centred * inverse
    return (normed * gain_row + shift_row, normed, inverse)


def norm_backward(grad_out, normed, inverse, gain_row):
    grad_normed = grad_out * gain_row
    inner_sum = jnp.mean(grad_normed, axis=-1, keepdims=True)
    along_norm = jnp.mean(grad_normed * normed, axis=-1, keepdims=True)
    return inverse * (grad_normed - inner_sum - normed * along_norm)


SCALE = HD ** (-0.5)
PAIR = 2 * HD
CHUNK = 768
VMEM_BYTES = 50 * 1024 * 1024


def head_part(block, head, part):
    at = (head * 3 + part) * HD
    return block[:, at : at + HD]


def attention_kernel(
    keep, x_ref, qkv_ref, qkv_bias_ref, column_ref, row_ref, output_ref, gains_ref, biases_ref, *rest
):
    if keep:
        first_ref, joined_ref, soft_ref, context_ref, normed_ref, inverse_ref, total = rest
    else:
        first_ref, total = rest
    step = pl.program_id(0)
    joined = (rows_by_units(x_ref[...], qkv_ref[...]) + qkv_bias_ref[0]).astype(BF16)
    same = column_ref[...] == row_ref[...]
    contexts = []
    for head in range(2):
        query = head_part(joined, head, 0) * jnp.asarray(SCALE, BF16)
        scores = jnp.where(same, rows_by_units(query, head_part(joined, head, 1)), MASKED)
        powers = jnp.exp(scores - jnp.max(scores, axis=-1, keepdims=True))
        soft = (powers * (1.0 / jnp.sum(powers, axis=-1, keepdims=True))).astype(BF16)
        contexts.append(plain(soft, head_part(joined, head, 2)))
        if keep:
            soft_ref[head] = soft
    context = jnp.concatenate(contexts, axis=1).astype(BF16)
    if keep:
        joined_ref[...] = joined
        context_ref[...] = context
    attended = plain(context, output_ref[...])

    @pl.when(step == 0)
    def _():
        total[...] = attended

    @pl.when(step > 0)
    def _():
        total[...] += attended

    @pl.when(step == pl.num_programs(0) - 1)
    def _():
        hidden = x_ref[...].astype(F32) + total[...] + biases_ref[0:1]
        first, normed, inverse = norm_forward(hidden, gains_ref[0:1], biases_ref[1:2])
        first_ref[...] = first
        if keep:
            normed_ref[...] = normed
            inverse_ref[...] = inverse


def units_kernel(keep, first_ref, expand_ref, expand_bias_ref, contract_ref, gains_ref, biases_ref, *rest):
    if keep:
        result_ref, active_ref, slope_ref, normed_ref, inverse_ref, total = rest
    else:
        result_ref, total = rest
    step = pl.program_id(0)
    pre_act = rows_by_units(first_ref[...].astype(BF16), expand_ref[...]) + expand_bias_ref[0]
    cdf = 0.5 * (1.0 + lax.erf(pre_act * 0.5**0.5))
    active = (pre_act * cdf).astype(BF16)
    if keep:
        density = jnp.exp(-0.5 * pre_act * pre_act) * 0.3989422804014327
        slope_ref[...] = (cdf + pre_act * density).astype(BF16)
        active_ref[...] = active
    returned = plain(active, contract_ref[...])

    @pl.when(step == 0)
    def _():
        total[...] = returned

    @pl.when(step > 0)
    def _():
        total[...] += returned

    @pl.when(step == pl.num_programs(0) - 1)
    def _():
        hidden = first_ref[...] + total[...] + biases_ref[2:3]
        result, normed, inverse = norm_forward(hidden, gains_ref[1:2], biases_ref[3:4])
        result_ref[...] = result.astype(BF16)
        if keep:
            normed_ref[...] = normed
            inverse_ref[...] = inverse


def units_back_kernel(
    sums,
    cotangent_ref,
    normed_two_ref,
    inverse_two_ref,
    normed_one_ref,
    inverse_one_ref,
    gains_ref,
    contract_ref,
    expand_ref,
    slope_ref,
    active_ref,
    first_ref,
    *rest,
):
    if sums:
        grad_one_ref, contract_grad_ref, expand_grad_ref, unit_sums_ref, row_sums_ref, returned, total = rest
    else:
        grad_one_ref, returned, total = rest
    step = pl.program_id(0)

    @pl.when(step == 0)
    def _():
        grad_two = norm_backward(
            cotangent_ref[...].astype(F32), normed_two_ref[...], inverse_two_ref[...], gains_ref[1:2]
        )
        returned[...] = grad_two.astype(BF16)
        total[...] = grad_two
        if sums:
            row_sums_ref[4:5] = jnp.sum(grad_two, axis=0, keepdims=True)

    grad_pre = (rows_by_units(returned[...], contract_ref[...]) * slope_ref[...].astype(F32)).astype(BF16)
    total[...] += plain(grad_pre, expand_ref[...])
    if sums:
        contract_grad_ref[...] = over_rows(active_ref[...], returned[...]).astype(BF16)
        expand_grad_ref[...] = over_rows(grad_pre, first_ref[...].astype(BF16)).astype(BF16)
        unit_sums_ref[0] = jnp.sum(grad_pre.astype(F32), axis=0, keepdims=True)

    @pl.when(step == pl.num_programs(0) - 1)
    def _():
        grad_first = total[...]
        normed = normed_one_ref[...]
        grad_one = norm_backward(grad_first, normed, inverse_one_ref[...], gains_ref[0:1])
        grad_one_ref[...] = grad_one
        if sums:
            cotangent = cotangent_ref[...].astype(F32)
            row_sums_ref[0:1] = jnp.sum(grad_first * normed, axis=0, keepdims=True)
            row_sums_ref[1:2] = jnp.sum(cotangent * normed_two_ref[...], axis=0, keepdims=True)
            row_sums_ref[2:3] = jnp.sum(grad_one, axis=0, keepdims=True)
            row_sums_ref[3:4] = jnp.sum(grad_first, axis=0, keepdims=True)
            row_sums_ref[5:6] = jnp.sum(cotangent, axis=0, keepdims=True)


def attention_back_kernel(
    sums, grad_one_ref, output_ref, joined_ref, soft_ref, qkv_ref, x_ref, context_ref, *rest
):
    if sums:
        grad_x_ref, qkv_grad_ref, output_grad_ref, joined_sums_ref, total = rest
    else:
        grad_x_ref, total = rest
    step = pl.program_id(0)

    @pl.when(step == 0)
    def _():
        total[...] = grad_one_ref[...]

    attended = grad_one_ref[...].astype(BF16)
    joined = joined_ref[...]
    grad_context = rows_by_units(attended, output_ref[...]).astype(BF16)
    pieces = []
    for head in range(2):
        grad_head = grad_context[:, head * HD : (head + 1) * HD]
        soft = soft_ref[head]
        soft_float = soft.astype(F32)
        grad_soft = rows_by_units(grad_head, head_part(joined, head, 2))
        inner = jnp.sum(grad_soft * soft_float, axis=-1, keepdims=True)
        grad_scores = (soft_float * (grad_soft - inner)).astype(BF16)
        pieces.append(plain(grad_scores, head_part(joined, head, 1)) * SCALE)
        pieces.append(over_rows(grad_scores, head_part(joined, head, 0)) * SCALE)
        pieces.append(over_rows(soft, grad_head))
    grad_joined = jnp.concatenate(pieces, axis=1).astype(BF16)
    total[...] += plain(grad_joined, qkv_ref[...])
    if sums:
        qkv_grad_ref[...] = over_rows(grad_joined, x_ref[...]).astype(BF16)
        output_grad_ref[...] = over_rows(context_ref[...], attended).astype(BF16)
        joined_sums_ref[0] = jnp.sum(grad_joined.astype(F32), axis=0, keepdims=True)

    @pl.when(step == pl.num_programs(0) - 1)
    def _():
        grad_x_ref[...] = total[...].astype(BF16)


def fixed(*shape):
    return pl.BlockSpec(shape, lambda i: (0,) * len(shape))


def down(rows, columns):
    return pl.BlockSpec((rows, columns), lambda i: (i, 0))


def across(rows, columns):
    return pl.BlockSpec((rows, columns), lambda i: (0, i))


def stacked(count, rows, columns):
    return pl.BlockSpec((count, rows, columns), lambda i: (i, 0, 0))


def shaped(shape, kind):
    return jax.ShapeDtypeStruct(shape, kind)


def run(kernel, steps, in_specs, outs, scratch, flops, args):
    return pl.pallas_call(
        kernel,
        grid=(steps,),
        in_specs=in_specs,
        out_specs=[spec for spec, _ in outs],
        out_shape=[shape for _, shape in outs],
        scratch_shapes=scratch,
        compiler_params=pltpu.CompilerParams(
            vmem_limit_bytes=VMEM_BYTES, dimension_semantics=("arbitrary",)
        ),
        cost_estimate=pl.CostEstimate(flops=flops, bytes_accessed=12_000_000, transcendentals=0),
    )(*args)


def layer_forward(keep, inputs, segment_ids, weights, smalls):
    qkv, output, expand, contract = weights
    qkv_bias, expand_bias, gains, biases = smalls
    rows, features = inputs.shape
    pairs = features // PAIR
    units = expand.shape[0]
    kept = lambda items: items if keep else []
    outs = [(fixed(rows, features), shaped((rows, features), F32))] + kept(
        [
            (across(rows, 3 * PAIR), shaped((rows, 3 * features), BF16)),
            (stacked(2, rows, rows), shaped((2 * pairs, rows, rows), BF16)),
            (across(rows, PAIR), shaped((rows, features), BF16)),
            (fixed(rows, features), shaped((rows, features), F32)),
            (fixed(rows, 1), shaped((rows, 1), F32)),
        ]
    )
    attention = run(
        partial(attention_kernel, keep),
        pairs,
        [
            fixed(rows, features),
            down(3 * PAIR, features),
            stacked(1, 1, 3 * PAIR),
            fixed(rows, 1),
            fixed(1, rows),
            down(PAIR, features),
            fixed(2, features),
            fixed(4, features),
        ],
        outs,
        [pltpu.VMEM((rows, features), F32)],
        8 * rows * features * features + 4 * rows * rows * features,
        (
            inputs,
            qkv,
            qkv_bias.reshape(pairs, 1, 3 * PAIR),
            segment_ids[:, None],
            segment_ids[None, :],
            output,
            gains,
            biases,
        ),
    )
    first = attention[0]
    outs = [(fixed(rows, features), shaped((rows, features), BF16))] + kept(
        [
            (across(rows, CHUNK), shaped((rows, units), BF16)),
            (across(rows, CHUNK), shaped((rows, units), BF16)),
            (fixed(rows, features), shaped((rows, features), F32)),
            (fixed(rows, 1), shaped((rows, 1), F32)),
        ]
    )
    middle = run(
        partial(units_kernel, keep),
        units // CHUNK,
        [
            fixed(rows, features),
            down(CHUNK, features),
            stacked(1, 1, CHUNK),
            down(CHUNK, features),
            fixed(2, features),
            fixed(4, features),
        ],
        outs,
        [pltpu.VMEM((rows, features), F32)],
        4 * rows * features * units,
        (first, expand, expand_bias.reshape(units // CHUNK, 1, CHUNK), contract, gains, biases),
    )
    return (middle[0], (inputs, *attention, *middle[1:]))


def layer_backward(sums, cotangent, weights, gains, saved):
    qkv, output, expand, contract = weights
    inputs, first, joined, soft, context, normed_one, inverse_one, active, slope, normed_two, inverse_two = saved
    rows, features = inputs.shape
    pairs = features // PAIR
    units = expand.shape[0]
    chunks = units // CHUNK
    summed = lambda items: items if sums else []
    whole = fixed(rows, features)
    outs = [(whole, shaped((rows, features), F32))] + summed(
        [
            (down(CHUNK, features), shaped((units, features), BF16)),
            (down(CHUNK, features), shaped((units, features), BF16)),
            (stacked(1, 1, CHUNK), shaped((chunks, 1, CHUNK), F32)),
            (fixed(6, features), shaped((6, features), F32)),
        ]
    )
    middle = run(
        partial(units_back_kernel, sums),
        chunks,
        [
            whole,
            whole,
            fixed(rows, 1),
            whole,
            fixed(rows, 1),
            fixed(2, features),
            down(CHUNK, features),
            down(CHUNK, features),
            across(rows, CHUNK),
            across(rows, CHUNK) if sums else pl.BlockSpec(memory_space=pl.ANY),
            whole if sums else pl.BlockSpec(memory_space=pl.ANY),
        ],
        outs,
        [pltpu.VMEM((rows, features), BF16), pltpu.VMEM((rows, features), F32)],
        (8 if sums else 4) * rows * features * units,
        (
            cotangent,
            normed_two,
            inverse_two,
            normed_one,
            inverse_one,
            gains,
            contract,
            expand,
            slope,
            active,
            first,
        ),
    )
    outs = [(whole, shaped((rows, features), BF16))] + summed(
        [
            (down(3 * PAIR, features), shaped((3 * features, features), BF16)),
            (down(PAIR, features), shaped((features, features), BF16)),
            (stacked(1, 1, 3 * PAIR), shaped((pairs, 1, 3 * PAIR), F32)),
        ]
    )
    attention = run(
        partial(attention_back_kernel, sums),
        pairs,
        [
            whole,
            down(PAIR, features),
            across(rows, 3 * PAIR),
            stacked(2, rows, rows),
            down(3 * PAIR, features),
            whole if sums else pl.BlockSpec(memory_space=pl.ANY),
            across(rows, PAIR) if sums else pl.BlockSpec(memory_space=pl.ANY),
        ],
        outs,
        [pltpu.VMEM((rows, features), F32)],
        (16 if sums else 8) * rows * features * features + 8 * rows * rows * features,
        (middle[0], output, joined, soft, qkv, inputs, context),
    )
    return (attention[0], attention[1:], middle[1:])


def shards(
    ends_in,
    segments,
    qkv_weight,
    qkv_bias,
    output_weight,
    expand_weight,
    expand_bias,
    contract_weight,
    norm_gains,
    row_biases,
):
    section = lax.axis_index("section")
    along = lax.axis_index("tensor")
    dp_count = lax.axis_size("dp")
    tensor_count = lax.axis_size("tensor")
    flat_count = dp_count * tensor_count
    features = ends_in.shape[-1]
    heads = features // HD
    bias_part = qkv_bias.shape[-1]
    unit_part = expand_bias.shape[-1]
    norm_part = norm_gains.shape[-1]
    cut_one = 2 * bias_part
    cut_two = cut_one + unit_part
    cut_three = cut_two + 2 * norm_part
    cut_end = cut_three + 4 * norm_part
    small_rows = -(-cut_end // (16 * features)) * 16
    padding = small_rows * features - cut_end

    packed = jnp.concatenate(
        [
            qkv_bias[0].reshape(-1),
            expand_bias[0],
            norm_gains[0].reshape(-1),
            row_biases[0].reshape(-1),
            jnp.zeros((padding,), BF16),
        ]
    ).reshape(small_rows, features)
    sources = (qkv_weight[0], output_weight[0], expand_weight[0], contract_weight[0], packed)
    gathered = lax.all_gather(jnp.concatenate(sources, axis=0), SHARDS, axis=0, tiled=False)
    own = lax.all_to_all(ends_in[0], "tensor", 0, 1, tiled=True)[0]
    parts = []
    at = 0
    for item in sources:
        parts.append(gathered[:, at : at + item.shape[0]].reshape(-1, features))
        at += item.shape[0]
    weights = tuple(parts[:4])
    packed = parts[4].reshape(flat_count, -1).astype(F32)
    biases_qv = packed[:, :cut_one].reshape(flat_count, 2, bias_part).transpose(1, 0, 2).reshape(2, heads, HD)
    qkv_bias_row = jnp.stack(
        [biases_qv[0], jnp.zeros((heads, HD), F32), biases_qv[1]], axis=1
    ).reshape(-1)
    expand_bias_row = packed[:, cut_one:cut_two].reshape(-1)
    gains = packed[:dp_count, cut_two:cut_three].reshape(dp_count, 2, norm_part).transpose(1, 0, 2).reshape(2, features)
    biases = packed[:dp_count, cut_three:cut_end].reshape(dp_count, 4, norm_part).transpose(1, 0, 2).reshape(4, features)
    smalls = (qkv_bias_row, expand_bias_row, gains, biases)
    segment_ids = lax.dynamic_index_in_dim(segments, along, 0, keepdims=False)[0]

    early_result, _ = layer_forward(False, own, segment_ids, weights, smalls)
    arriving = lax.ppermute(early_result, "section", [(0, 1)])
    inputs = jnp.where(section == 0, own, arriving)
    result, saved = layer_forward(True, inputs, segment_ids, weights, smalls)
    early_grad, _, _ = layer_backward(False, own, weights, gains, saved)
    arriving_grad = lax.ppermute(early_grad, "section", [(1, 0)])
    cotangent = jnp.where(section == 1, own, arriving_grad)
    grad_inputs, attention_grads, unit_grads = layer_backward(True, cotangent, weights, gains, saved)

    joined_sums = attention_grads[2].reshape(heads, 3, HD)
    joined_sums = jnp.stack([joined_sums[:, 0].reshape(-1), joined_sums[:, 2].reshape(-1)])
    norm_sums = unit_grads[3].reshape(6, dp_count, norm_part).transpose(1, 0, 2).reshape(1, dp_count, -1)
    small_grads = jnp.concatenate(
        [
            joined_sums.reshape(2, flat_count, bias_part).transpose(1, 0, 2).reshape(flat_count, -1),
            unit_grads[2].reshape(flat_count, unit_part),
            jnp.broadcast_to(norm_sums, (tensor_count, *norm_sums.shape[1:])).reshape(flat_count, -1),
            jnp.zeros((flat_count, padding), F32),
        ],
        axis=1,
    ).astype(BF16)
    grads = (attention_grads[0], attention_grads[1], unit_grads[1], unit_grads[0], small_grads)
    grads = jnp.concatenate([item.reshape(flat_count, -1, features) for item in grads], axis=1)
    summed = lax.psum_scatter(grads, SHARDS, scatter_dimension=0, tiled=True)[0].astype(F32)
    ends = jnp.where(section == 0, grad_inputs, result).reshape(ends_in.shape[1:])
    ends_out = lax.all_to_all(ends, "tensor", 0, 0, tiled=True).astype(F32)
    results = []
    at = 0
    for item in sources:
        results.append(summed[at : at + item.shape[0]])
        at += item.shape[0]
    small = results[4].reshape(-1)
    return (
        ends_out[None],
        results[0][None],
        small[:cut_one].reshape(1, 2, bias_part),
        results[1][None],
        results[2][None],
        small[None, cut_one:cut_two],
        results[3][None],
        small[cut_two:cut_three].reshape(1, 2, norm_part),
        small[cut_three:cut_end].reshape(1, 4, norm_part),
    )


def solution(mesh):
    rows = P("section", None, ("dp", "tensor"), None)
    units = P("section", SHARDS, None)
    biases = P("section", None, SHARDS)
    norms = P("section", None, "dp")
    vector = P("section", SHARDS)
    return jax.shard_map(
        shards,
        mesh=mesh,
        in_specs=(rows, P(None, "dp", None), units, biases, units, units, vector, units, norms, norms),
        out_specs=(rows, units, biases, units, units, vector, units, norms, norms),
        check_vma=False,
    )
```

time: 662 us -> 516 us (0.78); the launches traced: 652 us -> 515 us
  matrix products: 132 us -> 0 us
  Pallas kernels: 0 us -> 126 us
  blocking collectives: 142 us -> 21.8 us
  other arithmetic: 35 us -> 6.09 us
  local copies, waits for them, and re-layouts: 29 us -> 54.7 us
    pallas_call x0 -> x8, Pallas kernels: none -> 126 us  [run(): pl.pallas_call(kernel, grid=(steps,), in_specs=in_specs, out_specs=[spec...]
    dot_general x30 -> x0, matrix products: 117 us -> none  [the longest x8 40.4 us: rows_by_units(): lax.dot_general(left_side, right_side, (((1,), (1,)), ((), ())), preferre...]
    unnamed x1 -> x0, blocking collectives: 73.6 us -> none
    psum x1 -> x0, blocking collectives: 68.2 us -> none  [shards(): small_sums = lax.psum(small_grads, SHARDS)]
    reduce_scatter x4 -> x1, waiting for transfers between devices: 152 us -> 122 us  [shards(): lax.psum_scatter(grads, SHARDS, scatter_dimension=0, tiled=True)[0]]
    all_gather x4 -> x1, waiting for transfers between devices: 91.3 us -> 120 us  [shards(): lax.all_gather(jnp.concatenate(sources, axis=0), SHARDS, axis=0, tiled=Fa...]
    all_to_all x0 -> x1, blocking collectives: none -> 21.8 us  [shards(): ends_out = lax.all_to_all(ends, 'tensor', 0, 0, tiled=True).astype(F32)]
    slice x9 -> x14, local copies, waits for them, and re-layouts: 0.2 us -> 21.6 us  [the longest x3 13.7 us: shards(): parts.append(gathered[:, at:at + item.shape[0]].reshape(-1, features))]
  transfers between devices with their start and end apart: 12 -> 5, of which waited for: 6 -> 4; matrix products, arithmetic and copies ran while one was open for 14% -> 4% of each run, Pallas kernels for 0% -> 0%
where the time goes in v2:
time: 516 us; the launch traced here: 515 us
  waiting for transfers between devices  279 us (54%)
  Pallas kernels  126 us (24%)
  local copies, waits for them, and re-layouts  54.7 us (11%)
  blocking collectives  21.8 us (4%)
  between operations  14.4 us (3%)
  starting transfers between devices  12.1 us (2%)
  other arithmetic  6.09 us (1%)
    pallas_call x8, Pallas kernels, run(): pl.pallas_call(kernel, grid=(steps,), in_specs=in_specs, out_specs=[spec...  126 us
    reduce_scatter x1, waiting for transfers between devices, shards(): lax.psum_scatter(grads, SHARDS, scatter_dimension=0, tiled=True)[0]  122 us
    all_gather x1, waiting for transfers between devices, shards(): lax.all_gather(jnp.concatenate(sources, axis=0), SHARDS, axis=0, tiled=Fa...  120 us
    unnamed x62, local copies, waits for them, and re-layouts  25.6 us
    all_to_all x1, blocking collectives, shards(): ends_out = lax.all_to_all(ends, 'tensor', 0, 0, tiled=True).astype(F32)  21.8 us
    ppermute x1, waiting for transfers between devices, shards(): arriving_grad = lax.ppermute(early_grad, 'section', [(1, 0)])  20.9 us
    ppermute x1, waiting for transfers between devices, shards(): arriving = lax.ppermute(early_result, 'section', [(0, 1)])  16.3 us
    slice x3, local copies, waits for them, and re-layouts, shards(): parts.append(gathered[:, at:at + item.shape[0]].reshape(-1, features))  13.7 us
  transfers between devices with their start and end apart: 5, of which 4 were waited for; matrix products, arithmetic and copies ran while one was open for 4% of the time, Pallas kernels for 0%

profile of v2, /device:TPU:0, one launch (start us, length us, event | category | flops | bytes accessed | tf_op | source)
XLA Modules:
  0.0 515.0 jit_solution(5623199089317563284)
XLA Ops:
  15.1 6.3 %all-to-all-start = ((bf16[4,128,768]{2,1,0:T(8,128)(2,1)}), bf16[4,128,768]{2,1,0:T(8,128)(2,1)S(1)}, u32[]{:S(2)}, u32[]{:S(2)}) async-start(bf16[4,128,768]{2,1,0:T(8,128)(2,1)} %bitcast.81), calls=%async_computation | async-start | bytes 1572864 | tf_op jit(solution)/shard_map/all_to_all | solution.py:452
  22.4 120.1 %all-gather.3.cloned.1.call-done = bf16[9472,768]{1,0:T(8,128)(2,1)} async-done(((bf16[592,768]{1,0:T(8,128)(2,1)}), bf16[9472,768]{1,0:T(8,128)(2,1)}) %all-gather.3.cloned.1.call-update) | async-done | bytes 14549008 | tf_op jit(solution)/shard_map/all_gather | solution.py:451
  144.2 4.0 slice.101
  150.5 8.4 %fusion = (bf16[16,192,768]{2,1,0:T(8,128)(2,1)}, bf16[16,192,768]{2,1,0:T(8,128)(2,1)}) fusion(bf16[16,592,768]{2,1,0:T(8,128)(2,1)} %bitcast.61), kind=kLoop, calls=%fused_computation.26 | loop fusion | bytes 18874368 | tf_op jit(solution)/shard_map/slice | solution.py:456
  158.9 15.5 %shard_map.169.first_ref = f32[512,768]{1,0:T(8,128)S(1)} custom-call(bf16[512,768]{1,0:T(8,128)(2,1)S(1)} %bitcast.43, bf16[2304,768]{1,0:T(8,128)(2,1)} %bitcast.62, f32[6,1,384]{2,1,0:T(1,128)S(1)} %reshape_reshape.4.qkv_bias_ref, s32[512,1]{1,0:T(8,128)S(1)} %copy.27.column_ref, s32[1,512]{1,0:T(1,128)S(1)} %get-tuple-element.57.row_ref, ...), custom_call_target="tpu_custom_call" | custom-call | flops 3221225472 | bytes 12000000 | tf_op jit(solution)/shard_map/pallas_call | solution.py:250
  174.5 9.1 %shard_map.170 = bf16[512,768]{1,0:T(8,128)(2,1)S(1)} custom-call(f32[512,768]{1,0:T(8,128)S(1)} %shard_map.169.first_ref, bf16[3072,768]{1,0:T(8,128)(2,1)} %bitcast.54, f32[4,1,768]{2,1,0:T(1,128)S(1)} %reshape_reshape.10.expand_bias_ref, bf16[3072,768]{1,0:T(8,128)(2,1)} %bitcast.50, f32[2,768]{1,0:T(2,128)S(1)} %reshape.134.gains_ref, ...), custom_call_target="tpu_custom_call" | custom-call | flops 4831838208 | bytes 12000000 | tf_op jit(solution)/shard_map/pallas_call | solution.py:250
  183.6 4.3 collective-permute-start
  187.8 16.3 %collective-permute-done = bf16[512,768]{1,0:T(8,128)(2,1)} collective-permute-done((bf16[512,768]{1,0:T(8,128)(2,1)S(1)}, bf16[512,768]{1,0:T(8,128)(2,1)}, u32[]{:S(2)}, u32[]{:S(2)}) %collective-permute-start) | collective-permute-done | bytes 786464 | tf_op jit(solution)/shard_map/ppermute | solution.py:471
  206.7 18.2 %shard_map.171 = (f32[512,768]{1,0:T(8,128)}, bf16[512,2304]{1,0:T(8,128)(2,1)}, bf16[12,512,512]{2,1,0:T(8,128)(2,1)}, bf16[512,768]{1,0:T(8,128)(2,1)S(1)}, f32[512,768]{1,0:T(8,128)}, /*index=5*/f32[512,1]{1,0:T(8,128)S(1)}) custom-call(bf16[512,768]{1,0:T(8,128)(2,1)S(1)} %broadcast_select_fusion.2.x_ref, bf16[2304,768]{1,0:T(8,128)(2,1)} %bitcast.63, ...), custom_call_target="tpu_custom_call" | custom-call | flops 3221225472 | bytes 12000000 | tf_op jit(solution)/shard_map/pallas_call | solution.py:250
  224.9 12.2 %shard_map.172 = (bf16[512,768]{1,0:T(8,128)(2,1)S(1)}, bf16[512,3072]{1,0:T(8,128)(2,1)}, bf16[512,3072]{1,0:T(8,128)(2,1)}, f32[512,768]{1,0:T(8,128)S(1)}, f32[512,1]{1,0:T(8,128)S(1)}) custom-call(f32[512,768]{1,0:T(8,128)} %get-tuple-element.29.first_ref, bf16[3072,768]{1,0:T(8,128)(2,1)} %bitcast.55, f32[4,1,768]{2,1,0:T(1,128)S(1)} %copy-done.16, ...), custom_call_target="tpu_custom_call" | custom-call | flops 4831838208 | bytes 12000000 | tf_op jit(solution)/shard_map/pallas_call | solution.py:250
  239.1 11.2 %shard_map.173.grad_one_ref = f32[512,768]{1,0:T(8,128)S(1)} custom-call(bf16[512,768]{1,0:T(8,128)(2,1)S(1)} %bitcast.44, f32[512,768]{1,0:T(8,128)} %copy-done.2, f32[512,1]{1,0:T(8,128)S(1)} %get-tuple-element.31.inverse_two_ref, f32[512,768]{1,0:T(8,128)} %get-tuple-element.32.normed_one_ref, f32[512,1]{1,0:T(8,128)S(1)} %get-tuple-element.33.inverse_one_ref, ...), custom_call_target="tpu_custom_call" | custom-call | flops 4831838208 | bytes 12000000 | tf_op jit(solution)/shard_map/pallas_call | solution.py:250
  251.6 19.7 %shard_map.174 = bf16[512,768]{1,0:T(8,128)(2,1)} custom-call(f32[512,768]{1,0:T(8,128)} %copy-done, bf16[768,768]{1,0:T(8,128)(2,1)S(1)} %bitcast.47, bf16[512,2304]{1,0:T(8,128)(2,1)} %get-tuple-element.36.joined_ref, bf16[12,512,512]{2,1,0:T(8,128)(2,1)} %get-tuple-element.37.soft_ref, bf16[2304,768]{1,0:T(8,128)(2,1)} %bitcast.64, ...), custom_call_target="tpu_custom_call" | custom-call | flops 4026531840 | bytes 12000000 | tf_op jit(solution)/shard_map/pallas_call | solution.py:250
  271.3 1.5 collective-permute-start.1
  272.8 20.9 %collective-permute-done.1 = bf16[512,768]{1,0:T(8,128)(2,1)} collective-permute-done((bf16[512,768]{1,0:T(8,128)(2,1)}, bf16[512,768]{1,0:T(8,128)(2,1)}, u32[]{:S(2)}, u32[]{:S(2)}) %collective-permute-start.1) | collective-permute-done | bytes 786464 | tf_op jit(solution)/shard_map/ppermute | solution.py:475
  296.8 18.5 %shard_map.175 = (f32[512,768]{1,0:T(8,128)S(1)}, bf16[3072,768]{1,0:T(8,128)(2,1)}, bf16[3072,768]{1,0:T(8,128)(2,1)}, f32[4,1,768]{2,1,0:T(1,128)S(1)}, f32[6,768]{1,0:T(8,128)S(1)}) custom-call(bf16[512,768]{1,0:T(8,128)(2,1)S(1)} %broadcast_select_fusion.cotangent_ref, f32[512,768]{1,0:T(8,128)} %copy-done.2, f32[512,1]{1,0:T(8,128)S(1)} %copy-done.8, ...), custom_call_target="tpu_custom_call" | custom-call | flops 9663676416 | bytes 12000000 | tf_op jit(solution)/shard_map/pallas_call | solution.py:250
  316.5 22.1 %shard_map.176 = (bf16[512,768]{1,0:T(8,128)(2,1)S(1)}, bf16[2304,768]{1,0:T(8,128)(2,1)}, bf16[768,768]{1,0:T(8,128)(2,1)S(1)}, f32[6,1,384]{2,1,0:T(1,128)S(1)}) custom-call(f32[512,768]{1,0:T(8,128)} %copy-done.20, bf16[768,768]{1,0:T(8,128)(2,1)} %bitcast.48, bf16[512,2304]{1,0:T(8,128)(2,1)} %get-tuple-element.36.joined_ref, ...), custom_call_target="tpu_custom_call" | custom-call | flops 6442450944 | bytes 12000000 | tf_op jit(solution)/shard_map/pallas_call | solution.py:250
  341.4 4.2 constant_dynamic-update-slice_fusion.5
  346.7 2.6 constant_dynamic-update-slice_fusion.3
  349.3 2.6 constant_dynamic-update-slice_fusion.2
  353.9 21.8 %all_to_all.14 = bf16[4,128,768]{2,1,0:T(8,128)(2,1)S(1)} all-to-all(bf16[4,128,768]{2,1,0:T(8,128)(2,1)S(1)} %bitcast.73), channel_id=1, replica_groups=mesh['section'=2,'dp'=4,'tensor'=4] {'tensor'}, dimensions={0} | all-to-all | bytes 1572864 | tf_op jit(solution)/shard_map/all_to_all | solution.py:495
  376.9 122.1 %reduce-scatter.2.cloned.1.call-done = bf16[1,592,768]{2,1,0:T(8,128)(2,1)} async-done(((bf16[16,592,768]{2,1,0:T(8,128)(2,1)}), bf16[1,592,768]{2,1,0:T(8,128)(2,1)}) %reduce-scatter.2.cloned.1.call-update) | async-done | bytes 909328 | tf_op jit(solution)/shard_map/reduce_scatter | solution.py:493
  502.7 2.1 fusion.1
  504.8 1.7 slice.114
  506.6 1.6 slice.117
  (128 shorter events, 33.7 us)
Async XLA Ops:
  7.2 135.3 %all-gather.3.cloned.1.call-start = ((), (), s32[]{:S(2)}) async-start(), calls=%async_computation.4 | async-start | bytes 15458304 | tf_op jit(solution)/shard_map/all_gather | solution.py:451
  15.1 143.8 %all-to-all-start = ((bf16[4,128,768]{2,1,0:T(8,128)(2,1)}), bf16[4,128,768]{2,1,0:T(8,128)(2,1)S(1)}, u32[]{:S(2)}, u32[]{:S(2)}) async-start(bf16[4,128,768]{2,1,0:T(8,128)(2,1)} %bitcast.81), calls=%async_computation | async-start | bytes 1572864 | tf_op jit(solution)/shard_map/all_to_all | solution.py:452
  21.5 477.6 %reduce-scatter.2.cloned.1.call-start = ((), (), s32[]{:S(2)}) async-start(), calls=%async_computation.3 | async-start | bytes 15458304 | tf_op jit(solution)/shard_map/reduce_scatter | solution.py:493
  22.3 136.6 %copy-start.9 = (s32[512,1]{1,0:T(8,128)}, s32[512,1]{1,0:T(8,128)S(1)}, u32[]{:S(2)}) copy-start(s32[512,1]{1,0:T(8,128)S(1)} %copy.27.column_ref) | copy-start | bytes 6148
  149.5 102.1 %copy-start.1 = (bf16[16,48,768]{2,1,0:T(8,128)(2,1)}, bf16[16,48,768]{2,1,0:T(8,128)(2,1)S(1)}, u32[]{:S(2)}) copy-start(bf16[16,48,768]{2,1,0:T(8,128)(2,1)S(1)} %slice.106) | copy-start | bytes 3538948
  150.0 8.9 %copy-start.18 = (f32[6,1,384]{2,1,0:T(1,128)}, f32[6,1,384]{2,1,0:T(1,128)S(1)}, u32[]{:S(2)}) copy-start(f32[6,1,384]{2,1,0:T(1,128)S(1)} %reshape_reshape.4.qkv_bias_ref) | copy-start | bytes 27652
  150.4 24.0 %copy-start.12 = (f32[4,768]{1,0:T(4,128)}, f32[4,768]{1,0:T(4,128)S(1)}, u32[]{:S(2)}) copy-start(f32[4,768]{1,0:T(4,128)S(1)} %reshape.136.biases_ref) | copy-start | bytes 36868
  150.5 24.0 %copy-start.15 = (f32[4,1,768]{2,1,0:T(1,128)}, f32[4,1,768]{2,1,0:T(1,128)S(1)}, u32[]{:S(2)}) copy-start(f32[4,1,768]{2,1,0:T(1,128)S(1)} %reshape_reshape.10.expand_bias_ref) | copy-start | bytes 36868
  183.6 20.6 %collective-permute-start = (bf16[512,768]{1,0:T(8,128)(2,1)S(1)}, bf16[512,768]{1,0:T(8,128)(2,1)}, u32[]{:S(2)}, u32[]{:S(2)}) collective-permute-start(bf16[512,768]{1,0:T(8,128)(2,1)S(1)} %shard_map.170), channel_id=1, source_target_pairs={{0,16},{1,17},{2,18},{3,19},{4,20},{5,21},{6,22},{7,23},{8,24},{9,... | collective-permute-start | bytes 2359304 | tf_op jit(solution)/shard_map/ppermute | solution.py:471
  206.7 18.2 %copy-start.14 = (f32[4,768]{1,0:T(4,128)S(1)}, f32[4,768]{1,0:T(4,128)}, u32[]{:S(2)}) copy-start(f32[4,768]{1,0:T(4,128)} %copy-done.12) | copy-start | bytes 36868
  206.7 18.2 %copy-start.16 = (f32[4,1,768]{2,1,0:T(1,128)S(1)}, f32[4,1,768]{2,1,0:T(1,128)}, u32[]{:S(2)}) copy-start(f32[4,1,768]{2,1,0:T(1,128)} %copy-done.15) | copy-start | bytes 36868
  224.9 14.3 %copy-start.5 = (f32[512,1]{1,0:T(8,128)}, f32[512,1]{1,0:T(8,128)S(1)}, u32[]{:S(2)}) copy-start(f32[512,1]{1,0:T(8,128)S(1)} %get-tuple-element.33.inverse_one_ref) | copy-start | bytes 6148
  237.0 1.2 copy-start.2
  239.1 11.2 %copy-start.7 = (f32[512,1]{1,0:T(8,128)}, f32[512,1]{1,0:T(8,128)S(1)}, u32[]{:S(2)}) copy-start(f32[512,1]{1,0:T(8,128)S(1)} %get-tuple-element.31.inverse_two_ref) | copy-start | bytes 6148
  250.3 1.2 copy-start
  271.3 22.4 %collective-permute-start.1 = (bf16[512,768]{1,0:T(8,128)(2,1)}, bf16[512,768]{1,0:T(8,128)(2,1)}, u32[]{:S(2)}, u32[]{:S(2)}) collective-permute-start(bf16[512,768]{1,0:T(8,128)(2,1)} %shard_map.174), channel_id=1, source_target_pairs={{16,0},{17,1},{18,2},{19,3},{20,4},{21,5},{22,6},{23,7},{24,8},{25... | collective-permute-start | bytes 2359304 | tf_op jit(solution)/shard_map/ppermute | solution.py:475
  315.3 1.1 copy-start.20
  316.5 22.1 %copy-start.11 = (f32[6,768]{1,0:T(8,128)}, f32[6,768]{1,0:T(8,128)S(1)}, u32[]{:S(2)}) copy-start(f32[6,768]{1,0:T(8,128)S(1)} %get-tuple-element.48) | copy-start | bytes 55300
  316.5 22.1 %copy-start.17 = (f32[4,1,768]{2,1,0:T(1,128)}, f32[4,1,768]{2,1,0:T(1,128)S(1)}, u32[]{:S(2)}) copy-start(f32[4,1,768]{2,1,0:T(1,128)S(1)} %get-tuple-element.47) | copy-start | bytes 36868
  341.4 5.3 %slice-start.2 = ((s8[4718592]{0:T(1024)(128)(4,1)}), s8[4194304]{0:T(1024)(128)(4,1)S(1)}, s32[]{:S(2)}) async-start(s8[4718592]{0:T(1024)(128)(4,1)} %bitcast.69), calls=%async_computation.7 | async-start | bytes 8388608
  341.4 5.3 %slice-start.3 = ((s8[4718592]{0:T(1024)(128)(4,1)}), s8[524288]{0:T(1024)(128)(4,1)S(1)}, s32[]{:S(2)}) async-start(s8[4718592]{0:T(1024)(128)(4,1)} %bitcast.69), calls=%async_computation.8 | async-start | bytes 1048576
  345.5 3.7 slice-start
  346.7 2.6 slice-start.1
  352.6 1.1 copy-start.4
  (7 other events, 6.1 us)
Sparse Core Ops, SparseCore 0:
  15.3 127.1 all-gather.2
  352.8 146.1 reduce-scatter.1

commit v3 on v2

--- a/solution.py
+++ b/solution.py
@@ -448,15 +448,21 @@
         ]
     ).reshape(small_rows, features)
     sources = (qkv_weight[0], output_weight[0], expand_weight[0], contract_weight[0], packed)
-    gathered = lax.all_gather(jnp.concatenate(sources, axis=0), SHARDS, axis=0, tiled=False)
+    early_sources = (qkv_weight[0], output_weight[0], packed)
+    late_sources = (expand_weight[0], contract_weight[0])
+    early = lax.all_gather(jnp.concatenate(early_sources, axis=0), SHARDS, axis=0, tiled=False)
+    late_block = jnp.concatenate(late_sources, axis=0)
     own = lax.all_to_all(ends_in[0], "tensor", 0, 1, tiled=True)[0]
+    early, late_block, own = lax.optimization_barrier((early, late_block, own))
+    late = lax.all_gather(late_block, SHARDS, axis=0, tiled=False)
     parts = []
-    at = 0
-    for item in sources:
-        parts.append(gathered[:, at : at + item.shape[0]].reshape(-1, features))
-        at += item.shape[0]
-    weights = tuple(parts[:4])
-    packed = parts[4].reshape(flat_count, -1).astype(F32)
+    for block, items in ((early, early_sources), (late, late_sources)):
+        at = 0
+        for item in items:
+            parts.append(block[:, at : at + item.shape[0]].reshape(-1, features))
+            at += item.shape[0]
+    weights = (parts[0], parts[1], parts[3], parts[4])
+    packed = parts[2].reshape(flat_count, -1).astype(F32)
     biases_qv = packed[:, :cut_one].reshape(flat_count, 2, bias_part).transpose(1, 0, 2).reshape(2, heads, HD)
     qkv_bias_row = jnp.stack(
         [biases_qv[0], jnp.zeros((heads, HD), F32), biases_qv[1]], axis=1

time: 516 us -> 514 us (level)
    all_gather x1 -> x2, waiting for transfers between devices: 120 us -> 90.2 us  [the longest x1 56.9 us: shards(): late = lax.all_gather(late_block, SHARDS, axis=0, tiled=False)]
    all_to_all x1, waiting for transfers between devices: 0.01 us -> 27.8 us  [shards(): own = lax.all_to_all(ends_in[0], 'tensor', 0, 1, tiled=True)[0]]
    unnamed x62 -> x60, local copies, waits for them, and re-layouts: 25.6 us -> 21.8 us
  transfers between devices with their start and end apart: 5 -> 6, of which waited for: 4 -> 6; matrix products, arithmetic and copies ran while one was open for 4% -> 2% of each run, Pallas kernels for 0% -> 3%
where the time goes in v3:
time: 514 us; the launch traced here: 513 us
  waiting for transfers between devices  278 us (54%)
  Pallas kernels  127 us (25%)
  local copies, waits for them, and re-layouts  51.1 us (10%)
  blocking collectives  21.8 us (4%)
  between operations  14.1 us (3%)
  starting transfers between devices  12.2 us (2%)
  other arithmetic  9.68 us (2%)
    pallas_call x8, Pallas kernels, run(): pl.pallas_call(kernel, grid=(steps,), in_specs=in_specs, out_specs=[spec...  127 us
    reduce_scatter x1, waiting for transfers between devices, shards(): lax.psum_scatter(grads, SHARDS, scatter_dimension=0, tiled=True)[0]  122 us
    all_gather x1, waiting for transfers between devices, shards(): late = lax.all_gather(late_block, SHARDS, axis=0, tiled=False)  56.9 us
    all_gather x1, waiting for transfers between devices, shards(): lax.all_gather(jnp.concatenate(early_sources, axis=0), SHARDS, axis=0, ti...  33.3 us
    all_to_all x1, waiting for transfers between devices, shards(): own = lax.all_to_all(ends_in[0], 'tensor', 0, 1, tiled=True)[0]  27.8 us
    unnamed x60, local copies, waits for them, and re-layouts  21.8 us
    all_to_all x1, blocking collectives, shards(): ends_out = lax.all_to_all(ends, 'tensor', 0, 0, tiled=True).astype(F32)  21.8 us
    ppermute x1, waiting for transfers between devices, shards(): arriving_grad = lax.ppermute(early_grad, 'section', [(1, 0)])  20.9 us
  transfers between devices with their start and end apart: 6, of which 6 were waited for; matrix products, arithmetic and copies ran while one was open for 2% of the time, Pallas kernels for 3%

profile of v3, /device:TPU:0, one launch (start us, length us, event | category | flops | bytes accessed | tf_op | source)
XLA Modules:
  0.0 512.9 jit_solution(4142172085965890235)
XLA Ops:
  12.1 6.3 %all-to-all-start = ((bf16[4,128,768]{2,1,0:T(8,128)(2,1)}), bf16[4,128,768]{2,1,0:T(8,128)(2,1)S(1)}, u32[]{:S(2)}, u32[]{:S(2)}) async-start(bf16[4,128,768]{2,1,0:T(8,128)(2,1)} %bitcast.78), calls=%async_computation | async-start | bytes 1572864 | tf_op jit(solution)/shard_map/all_to_all | solution.py:455
  18.4 1.9 pad_maximum_fusion
  20.3 27.8 %all-to-all-done = bf16[4,128,768]{2,1,0:T(8,128)(2,1)S(1)} async-done(((bf16[4,128,768]{2,1,0:T(8,128)(2,1)}), bf16[4,128,768]{2,1,0:T(8,128)(2,1)S(1)}, u32[]{:S(2)}, u32[]{:S(2)}) %all-to-all-start) | async-done | bytes 786464 | tf_op jit(solution)/shard_map/all_to_all | solution.py:455
  48.2 33.3 %all-gather.5.cloned.1.call-done = bf16[3328,768]{1,0:T(8,128)(2,1)} async-done(((bf16[208,768]{1,0:T(8,128)(2,1)}), bf16[3328,768]{1,0:T(8,128)(2,1)}) %all-gather.5.cloned.1.call-update) | async-done | bytes 5111824 | tf_op jit(solution)/shard_map/all_gather | solution.py:453
  84.2 4.1 slice.78
  90.6 15.6 %shard_map.169.first_ref = f32[512,768]{1,0:T(8,128)S(1)} custom-call(bf16[512,768]{1,0:T(8,128)(2,1)S(1)} %bitcast.38, bf16[2304,768]{1,0:T(8,128)(2,1)} %bitcast.55, f32[6,1,384]{2,1,0:T(1,128)S(1)} %reshape_reshape.4.qkv_bias_ref, s32[512,1]{1,0:T(8,128)S(1)} %copy.27.column_ref, s32[1,512]{1,0:T(1,128)S(1)} %get-tuple-element.63.row_ref, ...), custom_call_target="tpu_custom_call" | custom-call | flops 3221225472 | bytes 12000000 | tf_op jit(solution)/shard_map/pallas_call | solution.py:250
  107.4 56.9 %all-gather.7.cloned.1.call-done = bf16[6144,768]{1,0:T(8,128)(2,1)} async-done(((bf16[384,768]{1,0:T(8,128)(2,1)}), bf16[6144,768]{1,0:T(8,128)(2,1)}) %all-gather.7.cloned.1.call-update) | async-done | bytes 9437200 | tf_op jit(solution)/shard_map/all_gather | solution.py:457
  164.4 8.5 %fusion = (bf16[16,192,768]{2,1,0:T(8,128)(2,1)}, bf16[16,192,768]{2,1,0:T(8,128)(2,1)}) fusion(bf16[16,384,768]{2,1,0:T(8,128)(2,1)} %bitcast.59), kind=kLoop, calls=%fused_computation.23 | loop fusion | bytes 18874368 | tf_op jit(solution)/shard_map/slice | solution.py:462
  172.9 9.1 %shard_map.170 = bf16[512,768]{1,0:T(8,128)(2,1)S(1)} custom-call(f32[512,768]{1,0:T(8,128)S(1)} %copy-done.21, bf16[3072,768]{1,0:T(8,128)(2,1)} %bitcast.51, f32[4,1,768]{2,1,0:T(1,128)S(1)} %reshape_reshape.10.expand_bias_ref, bf16[3072,768]{1,0:T(8,128)(2,1)} %bitcast.47, f32[2,768]{1,0:T(2,128)S(1)} %reshape.134.gains_ref, f32[4,768]{1,0:T(4,128)S(1)} %reshape.136.biases_ref), custom_call_target="tpu_custom_call" | custom-call | flops 4831838208 | bytes 12000000 | tf_op jit(solution)/shard_map/pallas_call | solution.py:250
  182.0 4.3 collective-permute-start
  186.3 16.3 %collective-permute-done = bf16[512,768]{1,0:T(8,128)(2,1)} collective-permute-done((bf16[512,768]{1,0:T(8,128)(2,1)S(1)}, bf16[512,768]{1,0:T(8,128)(2,1)}, u32[]{:S(2)}, u32[]{:S(2)}) %collective-permute-start) | collective-permute-done | bytes 786464 | tf_op jit(solution)/shard_map/ppermute | solution.py:477
  205.0 18.2 %shard_map.171 = (f32[512,768]{1,0:T(8,128)}, bf16[512,2304]{1,0:T(8,128)(2,1)}, bf16[12,512,512]{2,1,0:T(8,128)(2,1)}, bf16[512,768]{1,0:T(8,128)(2,1)S(1)}, f32[512,768]{1,0:T(8,128)}, /*index=5*/f32[512,1]{1,0:T(8,128)S(1)}) custom-call(bf16[512,768]{1,0:T(8,128)(2,1)S(1)} %broadcast_select_fusion.2.x_ref, bf16[2304,768]{1,0:T(8,128)(2,1)} %bitcast.56, ...), custom_call_target="tpu_custom_call" | custom-call | flops 3221225472 | bytes 12000000 | tf_op jit(solution)/shard_map/pallas_call | solution.py:250
  223.2 12.1 %shard_map.172 = (bf16[512,768]{1,0:T(8,128)(2,1)S(1)}, bf16[512,3072]{1,0:T(8,128)(2,1)}, bf16[512,3072]{1,0:T(8,128)(2,1)}, f32[512,768]{1,0:T(8,128)S(1)}, f32[512,1]{1,0:T(8,128)S(1)}) custom-call(f32[512,768]{1,0:T(8,128)} %get-tuple-element.35.first_ref, bf16[3072,768]{1,0:T(8,128)(2,1)} %bitcast.52, f32[4,1,768]{2,1,0:T(1,128)S(1)} %copy-done.16, ...), custom_call_target="tpu_custom_call" | custom-call | flops 4831838208 | bytes 12000000 | tf_op jit(solution)/shard_map/pallas_call | solution.py:250
  237.4 11.2 %shard_map.173.grad_one_ref = f32[512,768]{1,0:T(8,128)S(1)} custom-call(bf16[512,768]{1,0:T(8,128)(2,1)S(1)} %bitcast.40, f32[512,768]{1,0:T(8,128)} %copy-done.2, f32[512,1]{1,0:T(8,128)S(1)} %get-tuple-element.37.inverse_two_ref, f32[512,768]{1,0:T(8,128)} %get-tuple-element.38.normed_one_ref, f32[512,1]{1,0:T(8,128)S(1)} %get-tuple-element.39.inverse_one_ref, ...), custom_call_target="tpu_custom_call" | custom-call | flops 4831838208 | bytes 12000000 | tf_op jit(solution)/shard_map/pallas_call | solution.py:250
  249.7 19.6 %shard_map.174 = bf16[512,768]{1,0:T(8,128)(2,1)} custom-call(f32[512,768]{1,0:T(8,128)} %copy-done, bf16[768,768]{1,0:T(8,128)(2,1)S(1)} %bitcast.44, bf16[512,2304]{1,0:T(8,128)(2,1)} %get-tuple-element.42.joined_ref, bf16[12,512,512]{2,1,0:T(8,128)(2,1)} %get-tuple-element.43.soft_ref, bf16[2304,768]{1,0:T(8,128)(2,1)} %bitcast.57, ...), custom_call_target="tpu_custom_call" | custom-call | flops 4026531840 | bytes 12000000 | tf_op jit(solution)/shard_map/pallas_call | solution.py:250
  270.9 20.9 %collective-permute-done.1 = bf16[512,768]{1,0:T(8,128)(2,1)} collective-permute-done((bf16[512,768]{1,0:T(8,128)(2,1)}, bf16[512,768]{1,0:T(8,128)(2,1)}, u32[]{:S(2)}, u32[]{:S(2)}) %collective-permute-start.1) | collective-permute-done | bytes 786464 | tf_op jit(solution)/shard_map/ppermute | solution.py:481
  294.9 18.6 %shard_map.175 = (f32[512,768]{1,0:T(8,128)S(1)}, bf16[3072,768]{1,0:T(8,128)(2,1)}, bf16[3072,768]{1,0:T(8,128)(2,1)}, f32[4,1,768]{2,1,0:T(1,128)S(1)}, f32[6,768]{1,0:T(8,128)S(1)}) custom-call(bf16[512,768]{1,0:T(8,128)(2,1)S(1)} %broadcast_select_fusion.cotangent_ref, f32[512,768]{1,0:T(8,128)} %copy-done.2, f32[512,1]{1,0:T(8,128)S(1)} %copy-done.8, ...), custom_call_target="tpu_custom_call" | custom-call | flops 9663676416 | bytes 12000000 | tf_op jit(solution)/shard_map/pallas_call | solution.py:250
  314.7 22.1 %shard_map.176 = (bf16[512,768]{1,0:T(8,128)(2,1)S(1)}, bf16[2304,768]{1,0:T(8,128)(2,1)}, bf16[768,768]{1,0:T(8,128)(2,1)S(1)}, f32[6,1,384]{2,1,0:T(1,128)S(1)}) custom-call(f32[512,768]{1,0:T(8,128)} %copy-done.22, bf16[768,768]{1,0:T(8,128)(2,1)} %bitcast.45, bf16[512,2304]{1,0:T(8,128)(2,1)} %get-tuple-element.42.joined_ref, ...), custom_call_target="tpu_custom_call" | custom-call | flops 6442450944 | bytes 12000000 | tf_op jit(solution)/shard_map/pallas_call | solution.py:250
  339.6 4.2 constant_dynamic-update-slice_fusion.4
  344.9 2.6 constant_dynamic-update-slice_fusion.2
  347.5 2.6 constant_dynamic-update-slice_fusion.1
  352.1 21.8 %all_to_all.14 = bf16[4,128,768]{2,1,0:T(8,128)(2,1)S(1)} all-to-all(bf16[4,128,768]{2,1,0:T(8,128)(2,1)S(1)} %bitcast.70), channel_id=1, replica_groups=mesh['section'=2,'dp'=4,'tensor'=4] {'tensor'}, dimensions={0} | all-to-all | bytes 1572864 | tf_op jit(solution)/shard_map/all_to_all | solution.py:501
  375.1 122.1 %reduce-scatter.2.cloned.1.call-done = bf16[1,592,768]{2,1,0:T(8,128)(2,1)} async-done(((bf16[16,592,768]{2,1,0:T(8,128)(2,1)}), bf16[1,592,768]{2,1,0:T(8,128)(2,1)}) %reduce-scatter.2.cloned.1.call-update) | async-done | bytes 909328 | tf_op jit(solution)/shard_map/reduce_scatter | solution.py:499
  501.0 2.1 fusion.1
  (130 shorter events, 36.5 us)
Async XLA Ops:
  7.2 74.3 %all-gather.5.cloned.1.call-start = ((), (), s32[]{:S(2)}) async-start(), calls=%async_computation.4 | async-start | bytes 5431296 | tf_op jit(solution)/shard_map/all_gather | solution.py:453
  12.1 36.1 %all-to-all-start = ((bf16[4,128,768]{2,1,0:T(8,128)(2,1)}), bf16[4,128,768]{2,1,0:T(8,128)(2,1)S(1)}, u32[]{:S(2)}, u32[]{:S(2)}) async-start(bf16[4,128,768]{2,1,0:T(8,128)(2,1)} %bitcast.78), calls=%async_computation | async-start | bytes 1572864 | tf_op jit(solution)/shard_map/all_to_all | solution.py:455
  18.4 145.9 %all-gather.7.cloned.1.call-start = ((), (), s32[]{:S(2)}) async-start(), calls=%async_computation.5 | async-start | bytes 10027008 | tf_op jit(solution)/shard_map/all_gather | solution.py:457
  81.5 415.8 %reduce-scatter.2.cloned.1.call-start = ((), (), s32[]{:S(2)}) async-start(), calls=%async_computation.3 | async-start | bytes 15458304 | tf_op jit(solution)/shard_map/reduce_scatter | solution.py:499
  82.4 8.2 %copy-start.9 = (s32[512,1]{1,0:T(8,128)}, s32[512,1]{1,0:T(8,128)S(1)}, u32[]{:S(2)}) copy-start(s32[512,1]{1,0:T(8,128)S(1)} %copy.27.column_ref) | copy-start | bytes 6148
  89.6 160.1 %copy-start.1 = (bf16[16,48,768]{2,1,0:T(8,128)(2,1)}, bf16[16,48,768]{2,1,0:T(8,128)(2,1)S(1)}, u32[]{:S(2)}) copy-start(bf16[16,48,768]{2,1,0:T(8,128)(2,1)S(1)} %slice.83) | copy-start | bytes 3538948
  90.2 16.1 %copy-start.18 = (f32[6,1,384]{2,1,0:T(1,128)}, f32[6,1,384]{2,1,0:T(1,128)S(1)}, u32[]{:S(2)}) copy-start(f32[6,1,384]{2,1,0:T(1,128)S(1)} %reshape_reshape.4.qkv_bias_ref) | copy-start | bytes 27652
  90.5 82.3 %copy-start.12 = (f32[4,768]{1,0:T(4,128)}, f32[4,768]{1,0:T(4,128)S(1)}, u32[]{:S(2)}) copy-start(f32[4,768]{1,0:T(4,128)S(1)} %reshape.136.biases_ref) | copy-start | bytes 36868
  90.6 82.2 %copy-start.15 = (f32[4,1,768]{2,1,0:T(1,128)}, f32[4,1,768]{2,1,0:T(1,128)S(1)}, u32[]{:S(2)}) copy-start(f32[4,1,768]{2,1,0:T(1,128)S(1)} %reshape_reshape.10.expand_bias_ref) | copy-start | bytes 36868
  106.3 1.1 copy-start.20
  164.4 8.5 %copy-start.21 = (f32[512,768]{1,0:T(8,128)S(1)}, f32[512,768]{1,0:T(8,128)}, u32[]{:S(2)}) copy-start(f32[512,768]{1,0:T(8,128)} %copy-done.20) | copy-start | bytes 4718596
  182.0 20.6 %collective-permute-start = (bf16[512,768]{1,0:T(8,128)(2,1)S(1)}, bf16[512,768]{1,0:T(8,128)(2,1)}, u32[]{:S(2)}, u32[]{:S(2)}) collective-permute-start(bf16[512,768]{1,0:T(8,128)(2,1)S(1)} %shard_map.170), channel_id=1, source_target_pairs={{0,16},{1,17},{2,18},{3,19},{4,20},{5,21},{6,22},{7,23},{8,24},{9,... | collective-permute-start | bytes 2359304 | tf_op jit(solution)/shard_map/ppermute | solution.py:477
  205.0 18.2 %copy-start.14 = (f32[4,768]{1,0:T(4,128)S(1)}, f32[4,768]{1,0:T(4,128)}, u32[]{:S(2)}) copy-start(f32[4,768]{1,0:T(4,128)} %copy-done.12) | copy-start | bytes 36868
  205.0 18.2 %copy-start.16 = (f32[4,1,768]{2,1,0:T(1,128)S(1)}, f32[4,1,768]{2,1,0:T(1,128)}, u32[]{:S(2)}) copy-start(f32[4,1,768]{2,1,0:T(1,128)} %copy-done.15) | copy-start | bytes 36868
  223.2 14.2 %copy-start.5 = (f32[512,1]{1,0:T(8,128)}, f32[512,1]{1,0:T(8,128)S(1)}, u32[]{:S(2)}) copy-start(f32[512,1]{1,0:T(8,128)S(1)} %get-tuple-element.39.inverse_one_ref) | copy-start | bytes 6148
  235.3 1.1 copy-start.2
  237.4 11.2 %copy-start.7 = (f32[512,1]{1,0:T(8,128)}, f32[512,1]{1,0:T(8,128)S(1)}, u32[]{:S(2)}) copy-start(f32[512,1]{1,0:T(8,128)S(1)} %get-tuple-element.37.inverse_two_ref) | copy-start | bytes 6148
  269.4 22.4 %collective-permute-start.1 = (bf16[512,768]{1,0:T(8,128)(2,1)}, bf16[512,768]{1,0:T(8,128)(2,1)}, u32[]{:S(2)}, u32[]{:S(2)}) collective-permute-start(bf16[512,768]{1,0:T(8,128)(2,1)} %shard_map.174), channel_id=1, source_target_pairs={{16,0},{17,1},{18,2},{19,3},{20,4},{21,5},{22,6},{23,7},{24,8},{25... | collective-permute-start | bytes 2359304 | tf_op jit(solution)/shard_map/ppermute | solution.py:481
  314.7 22.1 %copy-start.11 = (f32[6,768]{1,0:T(8,128)}, f32[6,768]{1,0:T(8,128)S(1)}, u32[]{:S(2)}) copy-start(f32[6,768]{1,0:T(8,128)S(1)} %get-tuple-element.54) | copy-start | bytes 55300
  314.7 22.1 %copy-start.17 = (f32[4,1,768]{2,1,0:T(1,128)}, f32[4,1,768]{2,1,0:T(1,128)S(1)}, u32[]{:S(2)}) copy-start(f32[4,1,768]{2,1,0:T(1,128)S(1)} %get-tuple-element.53) | copy-start | bytes 36868
  339.6 5.3 %slice-start.2 = ((s8[4718592]{0:T(1024)(128)(4,1)}), s8[4194304]{0:T(1024)(128)(4,1)S(1)}, s32[]{:S(2)}) async-start(s8[4718592]{0:T(1024)(128)(4,1)} %bitcast.66), calls=%async_computation.8 | async-start | bytes 8388608
  339.6 5.3 %slice-start.3 = ((s8[4718592]{0:T(1024)(128)(4,1)}), s8[524288]{0:T(1024)(128)(4,1)S(1)}, s32[]{:S(2)}) async-start(s8[4718592]{0:T(1024)(128)(4,1)} %bitcast.66), calls=%async_computation.9 | async-start | bytes 1048576
  343.8 3.7 slice-start
  344.9 2.6 slice-start.1
  (9 other events, 8.6 us)
Sparse Core Ops, SparseCore 0:
  12.2 69.2 all-gather.4
  84.3 79.9 all-gather.6
  351.0 146.2 reduce-scatter.1
